TPU v7x, 32 devices: a whole 2x2x4 slice. The times are simulated.
32 devices in a mesh: axial: 8 (over z, core), circ: 4 (over y, x).
Axes of the slice: x: 2, y: 2, z: 4, core: 2. Of those that a mesh axis runs over, the one named last changes fastest.
Arguments:
- load_terms: float32 [8, 4, 128, 512], P('axial', 'circ'), may hold values from -19 to 19
- diffusivity: float32 [8, 4, 512], P('axial', 'circ'), may hold values from 0.1 to 10
- interface_diag: float32 [8, 4, 512], P('axial', 'circ'), may hold values from 4 to 8
- coupling: float32 [8, 4, 512, 512], P('axial', 'circ'), may hold values from -0.125 to 0.125
- interior_inverse: float32 [8, 4, 4, 128, 128], P('axial', 'circ'), may hold values from -1 to 3, as said below
- neumann_solve: float32 [8, 4, 512, 512], P('axial', 'circ'), may hold values from -1 to 3, as said below
- row_coarse: float32 [8, 8, 8], P('axial'), may hold values from -1 to 3, as said below
- lower_coef: float32 [8, 8], P('axial'), may hold values from 0.1 to 1
- upper_coef: float32 [8, 8], P('axial'), may hold values from 0.1 to 1
- face_order: int32 [8, 4, 512], P('axial', 'circ'), may hold values from 0 to 511, as said below
- primal_lists: int32 [8, 4, 8, 64], P('axial', 'circ'), may hold values from 0 to 511, as said below
Outputs:
- solution_field: float32 [8, 4, 128, 512], P('axial', 'circ')
- residual: float32 [8, 4, 128, 512], P('axial', 'circ')
Inputs may be any that keep to these rules, and one draw needn't show every extreme that they name: `face_order`: in each subdomain the values on face f (points f * 128 to f * 128 + 127) are those same numbers in some order; equal values on the two sides of a face name the same point. `primal_lists`: lists 2f and 2f + 1 together name every point of face f once. `interior_inverse`: symmetric in the last two dimensions. `neumann_solve`: symmetric in the last two dimensions. `row_coarse`: Symmetric, each diagonal entry larger than the sum of its row's other magnitudes.
All inputs are finite; a program needn't handle non-finite values.
Results may differ from a plain program's by a relative error of at most 0.0003.
Values sent between devices are 32-bit elements; how exact they have to be, the bound alone decides.
A program may use at most 64 MiB of HBM per device.

v0:
```python
import jax
import jax.numpy as jnp
from jax import lax
from jax.sharding import PartitionSpec as P

ITERS = 3


def with_halo(block, sides, width, periodic):
    for axis, dim in sides:
        count = lax.axis_size(axis)
        forward = [(i, i + 1) for i in range(count - 1)]
        if periodic:
            forward.append((count - 1, 0))
        backward = [(target, source) for source, target in forward]
        low = lax.ppermute(
            lax.slice_in_dim(block, block.shape[dim] - width, None, axis=dim), axis, forward
        )
        high = lax.ppermute(lax.slice_in_dim(block, 0, width, axis=dim), axis, backward)
        block = jnp.concatenate([low, block, high], axis=dim)
    return block


def invert_order(order):
    size = order.shape[0]
    return jnp.zeros((size,), jnp.int32).at[order].set(jnp.arange(size, dtype=jnp.int32))


def assemble(values, order, inverse):
    width = order.shape[0] // 4
    shared = jnp.take(values, inverse, axis=-1)
    south = shared[..., :width]
    north = shared[..., width : 2 * width]
    west = shared[..., 2 * width : 3 * width]
    east = shared[..., 3 * width :]
    axial_pair = with_halo(jnp.stack([south, north]), (("axial", 0),), 1, False)
    circ_pair = with_halo(jnp.stack([west, east]), (("circ", 0),), 1, True)
    below = axial_pair[0]
    above = axial_pair[3]
    left_side = circ_pair[0]
    right_side = circ_pair[3]
    summed = jnp.concatenate(
        [south + below, north + above, west + left_side, east + right_side], axis=-1
    )
    return jnp.take(summed, order, axis=-1)


def forward_step(carry, inputs):
    factor, value = inputs
    carry = factor * carry + (1.0 - factor) * value
    return (carry, carry)


def top_level(row_total, lower_local, upper_local):
    all_rows, all_lower, all_upper = (
        lax.all_gather(row_total[None], "axial", axis=0, tiled=True),
        lax.all_gather(lower_local, "axial", axis=0, tiled=True),
        lax.all_gather(upper_local, "axial", axis=0, tiled=True),
    )
    start = jnp.zeros_like(row_total)
    _, smoothed = lax.scan(forward_step, start, (all_lower[:, None, :], all_rows))
    _, tops = lax.scan(forward_step, start, (all_upper[:, None, :], smoothed), reverse=True)
    return lax.dynamic_index_in_dim(tops, lax.axis_index("axial"), 0, keepdims=False)


def local(
    load_terms,
    diffusivity,
    interface_diag,
    coupling,
    interior_inverse,
    neumann_solve,
    row_coarse,
    lower_coef,
    upper_coef,
    face_order,
    primal_lists,
):
    highest = lax.Precision.HIGHEST
    rhs_local = load_terms[0, 0]
    rho_local = diffusivity[0, 0]
    diag_local = interface_diag[0, 0]
    couple_local = coupling[0, 0]
    blocks_local = interior_inverse[0, 0]
    neumann_local = neumann_solve[0, 0]
    coarse_local = row_coarse[0]
    order = face_order[0, 0]
    lists = primal_lists[0, 0]
    points = order.shape[0]
    width = points // 4
    count_rhs = rhs_local.shape[0]
    block_count = blocks_local.shape[0]
    block_size = blocks_local.shape[1]
    list_len = lists.shape[1]
    inverse = invert_order(order)
    lower_flag = (lax.axis_index("axial") > 0).astype(jnp.float32)
    upper_flag = (lax.axis_index("axial") < lax.axis_size("axial") - 1).astype(jnp.float32)
    keep = jnp.concatenate(
        [
            jnp.full((width,), 1.0, jnp.float32) * lower_flag,
            jnp.full((width,), 1.0, jnp.float32) * upper_flag,
            jnp.ones((2 * width,), jnp.float32),
        ]
    )
    share = rho_local / assemble(rho_local, order, inverse)
    positions = jnp.arange(points, dtype=jnp.int32)
    averaging = (
        jnp.sum((lists[:, :, None] == positions[None, None, :]).astype(jnp.float32), axis=1)
        / list_len
    )

    def precondition(residual):
        weighted = share * residual
        local_part = jnp.dot(weighted, neumann_local, precision=highest)
        primal = lax.dot_general(weighted, averaging, (((1,), (1,)), ((), ())), precision=highest)
        row_total = lax.psum(primal, "circ")
        row_part = jnp.dot(row_total, coarse_local, precision=highest)
        top_part = top_level(row_total, lower_coef, upper_coef)
        coarse_part = jnp.dot(row_part + top_part, averaging, precision=highest)
        return assemble(share * (local_part + coarse_part), order, inverse) * keep

    def inner_product(first, second):
        return 0.5 * lax.psum(jnp.sum(first * second, axis=1), ("axial", "circ"))

    residual = assemble(rhs_local, order, inverse) * keep
    solution_field = jnp.zeros_like(residual)
    precond = precondition(residual)
    direction = precond
    rz_value = inner_product(residual, precond)
    for iteration in range(ITERS):
        inner = jnp.dot(direction, couple_local, precision=highest)
        blocked = inner.reshape(count_rhs, block_count, block_size)
        solved = jnp.einsum("rnk,nkl->rnl", blocked, blocks_local, precision=highest).reshape(
            count_rhs, block_count * block_size
        )
        back = lax.dot_general(solved, couple_local, (((1,), (1,)), ((), ())), precision=highest)
        image = assemble(diag_local * direction - back, order, inverse) * keep
        alpha = rz_value / inner_product(direction, image)
        solution_field = solution_field + alpha[:, None] * direction
        residual = residual - alpha[:, None] * image
        if iteration + 1 < ITERS:
            precond = precondition(residual)
            new_value = inner_product(residual, precond)
            direction = precond + (new_value / rz_value)[:, None] * direction
            rz_value = new_value
    return (solution_field[None, None], residual[None, None])


def solution(mesh):
    in_specs = (
        P("axial", "circ", None, None),
        P("axial", "circ", None),
        P("axial", "circ", None),
        P("axial", "circ", None, None),
        P("axial", "circ", None, None, None),
        P("axial", "circ", None, None),
        P("axial", None, None),
        P("axial", None),
        P("axial", None),
        P("axial", "circ", None),
        P("axial", "circ", None, None),
    )
    out_specs = (P("axial", "circ", None, None), P("axial", "circ", None, None))
    return jax.shard_map(local, mesh=mesh, in_specs=in_specs, out_specs=out_specs, check_vma=False)
```

profile of v0, /device:TPU:0, one launch (start us, length us, event | category | flops | bytes accessed | tf_op | source)
XLA Modules:
  0.0 496.4 jit_solution(10017897956692346555)
XLA Ops:
  1.4 2.4 scatter_custom_fusion
  4.6 3.5 gather_fusion.2
  9.4 2.4 collective-permute-start
  11.8 4.6 collective-permute-start.4
  18.0 1.3 collective-permute-start.5
  19.3 1.5 collective-permute-start.6
  20.9 1.4 collective-permute-start.7
  22.3 12.6 %all-gather.4 = f32[8,1,8]{2,1,0:T(1,128)S(1)} all-gather(f32[1,1,8]{2,1,0:T(1,128)S(1)} %bitcast.378), channel_id=1, replica_groups=mesh['axial'=8,'circ'=4] {'axial'}, dimensions={0}, use_global_device_ids=true | all-gather | bytes 288 | tf_op jit(solution)/shard_map/all_gather | solution.py:57
  35.6 8.6 %all-gather.3 = f32[8,1,8]{2,1,0:T(1,128)S(1)} all-gather(f32[1,1,8]{2,1,0:T(1,128)S(1)} %bitcast.379), channel_id=1, replica_groups=mesh['axial'=8,'circ'=4] {'axial'}, dimensions={0}, use_global_device_ids=true | all-gather | bytes 288 | tf_op jit(solution)/shard_map/all_gather | solution.py:58
  44.2 3.5 gather_fusion.3
  47.8 1.3 collective-permute-start.1
  49.8 2.2 collective-permute-start.3
  52.1 2.8 collective-permute-done.2
  54.8 1.5 collective-permute-done.3
  57.8 9.1 %psum.63 = f32[128,8]{0,1:T(8,128)S(1)} all-reduce(f32[128,8]{0,1:T(8,128)S(1)} %fusion.42), channel_id=1, replica_groups=mesh['axial'=8,'circ'=4] {'circ'}, use_global_device_ids=true, to_apply=%region_2.0 | all-reduce | flops 1024 | bytes 8192 | tf_op jit(solution)/shard_map/psum | solution.py:116
  66.9 14.8 %all-gather = f32[1024,8]{0,1:T(8,128)S(1)} all-gather(f32[128,8]{0,1:T(8,128)S(1)} %psum.63), channel_id=2, replica_groups=mesh['axial'=8,'circ'=4] {'axial'}, dimensions={0}, use_global_device_ids=true | all-gather | bytes 36864 | tf_op jit(solution)/shard_map/all_gather | solution.py:56
  85.7 2.3 collective-permute-start.8
  89.6 2.9 collective-permute-start.11
  94.1 1.6 collective-permute-done.10
  97.6 1.6 gather_fusion.5
  102.8 2.0 convolution_subtract_fusion.2
  105.8 1.6 gather_fusion.6
  108.6 4.7 collective-permute-start.12
  116.2 2.9 collective-permute-start.15
  119.1 3.1 collective-permute-done.14
  122.2 1.4 collective-permute-done.15
  124.6 1.6 gather_fusion.7
  126.2 1.8 copy.74
  129.3 40.9 %all-reduce = (f32[128]{0:T(128)S(1)}, f32[128]{0:T(128)S(1)}) all-reduce(f32[128]{0:T(128)S(1)} %get-tuple-element.509, f32[128]{0:T(128)S(1)} %get-tuple-element.508), channel_id=1, replica_groups=mesh['axial'=8,'circ'=4] {'axial','circ'}, use_global_device_ids=true, to_apply=%region_10.13 | all-reduce | flops 256 | bytes 2048 | tf_op jit(solution)/shard_map/psum | solution.py:123
  173.3 10.5 %psum.66 = f32[128,8]{0,1:T(8,128)S(1)} all-reduce(f32[128,8]{0,1:T(8,128)S(1)} %fusion.39), channel_id=1, replica_groups=mesh['axial'=8,'circ'=4] {'circ'}, use_global_device_ids=true, to_apply=%region_11.14 | all-reduce | flops 1024 | bytes 8192 | tf_op jit(solution)/shard_map/psum | solution.py:116
  183.8 14.0 %all-gather.1 = f32[1024,8]{0,1:T(8,128)S(1)} all-gather(f32[128,8]{0,1:T(8,128)S(1)} %psum.66), channel_id=3, replica_groups=mesh['axial'=8,'circ'=4] {'axial'}, dimensions={0}, use_global_device_ids=true | all-gather | bytes 36864 | tf_op jit(solution)/shard_map/all_gather | solution.py:56
  199.1 5.4 %while.93 = (s32[]{:T(128)}, f32[128,8]{0,1:T(8,128)S(1)}, f32[8,128,8]{1,2,0:T(8,128)}, f32[8,1,8]{2,1,0:T(1,128)S(1)}, f32[8,128,8]{1,2,0:T(8,128)S(1)}, /*index=5*/s32[]{:T(128)}, s32[]{:T(128)}, s32[]{:T(128)}) while((s32[]{:T(128)}, f32[128,8]{0,1:T(8,128)S(1)}, f32[8,128,8]{1,2,0:T(8,128)}, f32[8,1,8]{2,1,0:T(1,128)S(1)}, ...), condition=%wide.region_15.18_spmd.clone, body=%wide.region_14.17_spmd.clone.sunk | while | flops 4108 | bytes 16659 | solution.py:62
  207.5 1.6 gather_fusion.8
  210.3 2.2 collective-permute-start.16
  213.4 1.3 collective-permute-start.17
  214.8 2.9 collective-permute-start.19
  217.7 2.8 collective-permute-done.18
  221.2 1.6 gather_fusion.9
  222.9 1.8 copy.76
  225.8 41.3 %psum.67 = f32[128]{0:T(128)S(1)} all-reduce(f32[128]{0:T(128)S(1)} %multiply_reduce_fusion.3), channel_id=1, replica_groups=mesh['axial'=8,'circ'=4] {'axial','circ'}, use_global_device_ids=true, to_apply=%region_17.20 | all-reduce | flops 128 | bytes 1024 | tf_op jit(solution)/shard_map/psum | solution.py:123
  270.0 2.0 convolution_subtract_fusion.1
  273.1 1.6 gather_fusion.10
  275.9 1.3 collective-permute-start.20
  280.0 2.3 collective-permute-start.22
  284.2 1.3 collective-permute-done.22
  285.5 1.5 collective-permute-done.23
  288.0 1.6 gather_fusion.11
  289.6 1.8 copy.80
  292.5 44.1 %psum.68 = f32[128]{0:T(128)S(1)} all-reduce(f32[128]{0:T(128)S(1)} %multiply_reduce_fusion.2), channel_id=1, replica_groups=mesh['axial'=8,'circ'=4] {'axial','circ'}, use_global_device_ids=true, to_apply=%region_19.22 | all-reduce | flops 128 | bytes 1024 | tf_op jit(solution)/shard_map/psum | solution.py:123
  339.2 10.5 %psum.69 = f32[128,8]{0,1:T(8,128)S(1)} all-reduce(f32[128,8]{0,1:T(8,128)S(1)} %fusion.36), channel_id=1, replica_groups=mesh['axial'=8,'circ'=4] {'circ'}, use_global_device_ids=true, to_apply=%region_20.23 | all-reduce | flops 1024 | bytes 8192 | tf_op jit(solution)/shard_map/psum | solution.py:116
  349.7 14.0 %all-gather.2 = f32[1024,8]{0,1:T(8,128)S(1)} all-gather(f32[128,8]{0,1:T(8,128)S(1)} %psum.69), channel_id=4, replica_groups=mesh['axial'=8,'circ'=4] {'axial'}, dimensions={0}, use_global_device_ids=true | all-gather | bytes 36864 | tf_op jit(solution)/shard_map/all_gather | solution.py:56
  364.9 5.4 %while.95 = (s32[]{:T(128)}, f32[128,8]{0,1:T(8,128)S(1)}, f32[8,128,8]{1,2,0:T(8,128)}, f32[8,1,8]{2,1,0:T(1,128)S(1)}, f32[8,128,8]{1,2,0:T(8,128)S(1)}, /*index=5*/s32[]{:T(128)}, s32[]{:T(128)}, s32[]{:T(128)}) while((s32[]{:T(128)}, f32[128,8]{0,1:T(8,128)S(1)}, f32[8,128,8]{1,2,0:T(8,128)}, f32[8,1,8]{2,1,0:T(1,128)S(1)}, ...), condition=%wide.region_24.27_spmd.clone, body=%wide.region_23.26_spmd.clone.sunk | while | flops 4108 | bytes 16659 | solution.py:62
  373.4 1.6 gather_fusion.12
  376.1 2.2 collective-permute-start.24
  379.2 1.3 collective-permute-start.25
  380.6 2.9 collective-permute-start.27
  383.5 2.7 collective-permute-done.26
  386.9 1.6 gather_fusion.13
  388.6 1.8 copy.82
  391.5 41.7 %psum.70 = f32[128]{0:T(128)S(1)} all-reduce(f32[128]{0:T(128)S(1)} %multiply_reduce_fusion.1), channel_id=1, replica_groups=mesh['axial'=8,'circ'=4] {'axial','circ'}, use_global_device_ids=true, to_apply=%region_26.29 | all-reduce | flops 128 | bytes 1024 | tf_op jit(solution)/shard_map/psum | solution.py:123
  438.8 1.3 collective-permute-start.28
  442.3 2.3 collective-permute-start.30
  447.5 1.5 collective-permute-done.31
  451.2 44.2 %psum.71 = f32[128]{0:T(128)S(1)} all-reduce(f32[128]{0:T(128)S(1)} %multiply_reduce_fusion), channel_id=1, replica_groups=mesh['axial'=8,'circ'=4] {'axial','circ'}, use_global_device_ids=true, to_apply=%region_28.31 | all-reduce | flops 128 | bytes 1024 | tf_op jit(solution)/shard_map/psum | solution.py:123
  (310 shorter events, 87.8 us)
Async XLA Ops:
  0.6 82.3 %copy-start = (f32[1,1,512,512]{3,2,1,0:T(8,128)S(1)}, f32[1,1,512,512]{3,2,1,0:T(8,128)}, u32[]{:S(2)}) copy-start(f32[1,1,512,512]{3,2,1,0:T(8,128)} %param.32) | copy-start | bytes 3145732
  3.9 0.7 copy-start.1
  4.6 3.5 copy-start.20
  9.4 38.3 %collective-permute-start = (f32[1,128,128]{1,2,0:T(8,128)S(1)}, f32[1,128,128]{1,2,0:T(8,128)S(1)}, u32[]{:S(2)}, u32[]{:S(2)}) collective-permute-start(f32[1,128,128]{1,2,0:T(8,128)S(1)} %slice_bitcast_fusion.26), channel_id=1, source_target_pairs={{0,4},{4,8},{8,12},{12,16},{16,20},{20,24},{24,28},{1,5},{5,9},{9,... | collective-permute-start | bytes 196616 | tf_op jit(solution)/shard_map/ppermute | solution.py:16
  11.8 6.2 %collective-permute-start.4 = (f32[1,128]{1,0:T(1,128)S(1)}, f32[1,128]{1,0:T(1,128)S(1)}, u32[]{:S(2)}, u32[]{:S(2)}) collective-permute-start(f32[1,128]{1,0:T(1,128)S(1)} %slice_bitcast_fusion.30), channel_id=1, source_target_pairs={{0,4},{4,8},{8,12},{12,16},{16,20},{20,24},{24,28},{1,5},{5,9},{9,... | collective-permute-start | bytes 1544 | tf_op jit(solution)/shard_map/ppermute | solution.py:16
  16.4 0.7 copy-start.21
  17.1 0.7 copy-start.23
  18.0 26.2 %collective-permute-start.5 = (f32[1,128]{1,0:T(1,128)S(1)}, f32[1,128]{1,0:T(1,128)S(1)}, u32[]{:S(2)}, u32[]{:S(2)}) collective-permute-start(f32[1,128]{1,0:T(1,128)S(1)} %get-tuple-element.652), channel_id=1, source_target_pairs={{4,0},{8,4},{12,8},{16,12},{20,16},{24,20},{28,24},{5,1},{9,5},{13... | collective-permute-start | bytes 1544 | tf_op jit(solution)/shard_map/ppermute | solution.py:19
  19.3 24.9 %collective-permute-start.6 = (f32[1,128]{1,0:T(1,128)S(1)}, f32[1,128]{1,0:T(1,128)S(1)}, u32[]{:S(2)}, u32[]{:S(2)}) collective-permute-start(f32[1,128]{1,0:T(1,128)S(1)} %get-tuple-element.654), channel_id=1, source_target_pairs={{0,1},{1,2},{2,3},{3,0},{4,5},{5,6},{6,7},{7,4},{8,9},{9,10},{10,1... | collective-permute-start | bytes 1544 | tf_op jit(solution)/shard_map/ppermute | solution.py:16
  20.9 1.4 copy-start.24
  20.9 23.3 %collective-permute-start.7 = (f32[1,128]{1,0:T(1,128)S(1)}, f32[1,128]{1,0:T(1,128)S(1)}, u32[]{:S(2)}, u32[]{:S(2)}) collective-permute-start(f32[1,128]{1,0:T(1,128)S(1)} %get-tuple-element.653), channel_id=1, source_target_pairs={{1,0},{2,1},{3,2},{0,3},{5,4},{6,5},{7,6},{4,7},{9,8},{10,9},{11,1... | collective-permute-start | bytes 1544 | tf_op jit(solution)/shard_map/ppermute | solution.py:19
  34.9 0.7 copy-start.25
  47.8 4.3 collective-permute-start.1
  49.1 5.8 %collective-permute-start.2 = (f32[1,128,128]{1,2,0:T(8,128)S(1)}, f32[1,128,128]{1,2,0:T(8,128)S(1)}, u32[]{:S(2)}, u32[]{:S(2)}) collective-permute-start(f32[1,128,128]{1,2,0:T(8,128)S(1)} %get-tuple-element.645), channel_id=1, source_target_pairs={{0,1},{1,2},{2,3},{3,0},{4,5},{5,6},{6,7},{7,4},{8,9},{9,10},{10,1... | collective-permute-start | bytes 196616 | tf_op jit(solution)/shard_map/ppermute | solution.py:16
  49.8 6.5 %collective-permute-start.3 = (f32[1,128,128]{1,2,0:T(8,128)S(1)}, f32[1,128,128]{1,2,0:T(8,128)S(1)}, u32[]{:S(2)}, u32[]{:S(2)}) collective-permute-start(f32[1,128,128]{1,2,0:T(8,128)S(1)} %get-tuple-element.644), channel_id=1, source_target_pairs={{1,0},{2,1},{3,2},{0,3},{5,4},{6,5},{7,6},{4,7},{9,8},{10,9},{11,1... | collective-permute-start | bytes 196616 | tf_op jit(solution)/shard_map/ppermute | solution.py:19
  57.5 25.4 %copy-start.13 = (f32[512,128]{0,1:T(8,128)}, f32[512,128]{0,1:T(8,128)S(1)}, u32[]{:S(2)}) copy-start(f32[512,128]{0,1:T(8,128)S(1)} %copy.68) | copy-start | bytes 786436
  82.9 0.8 copy-start.26
  85.5 8.3 %copy-start.2 = (f32[1,1,512,512]{3,2,1,0:T(8,128)S(1)}, f32[1,1,512,512]{3,2,1,0:T(8,128)}, u32[]{:S(2)}) copy-start(f32[1,1,512,512]{3,2,1,0:T(8,128)} %param.30) | copy-start | bytes 3145732
  85.7 3.2 collective-permute-start.8
  89.6 6.1 %collective-permute-start.10 = (f32[1,128,128]{1,2,0:T(8,128)}, f32[1,128,128]{1,2,0:T(8,128)}, u32[]{:S(2)}, u32[]{:S(2)}) collective-permute-start(f32[1,128,128]{1,2,0:T(8,128)} %get-tuple-element.638), channel_id=1, source_target_pairs={{0,1},{1,2},{2,3},{3,0},{4,5},{5,6},{6,7},{7,4},{8,9},{9,10},{10,1... | collective-permute-start | bytes 196616 | tf_op jit(solution)/shard_map/ppermute | solution.py:16
  89.6 7.1 %collective-permute-start.11 = (f32[1,128,128]{1,2,0:T(8,128)}, f32[1,128,128]{1,2,0:T(8,128)}, u32[]{:S(2)}, u32[]{:S(2)}) collective-permute-start(f32[1,128,128]{1,2,0:T(8,128)} %get-tuple-element.637), channel_id=1, source_target_pairs={{1,0},{2,1},{3,2},{0,3},{5,4},{6,5},{7,6},{4,7},{9,8},{10,9},{11,1... | collective-permute-start | bytes 196616 | tf_op jit(solution)/shard_map/ppermute | solution.py:19
  92.5 4.1 collective-permute-start.9
  100.3 1.8 copy-start.3
  100.3 1.1 copy-start.17
  102.1 0.7 copy-start.22
  108.6 5.6 %collective-permute-start.12 = (f32[1,128,128]{1,2,0:T(8,128)S(1)}, f32[1,128,128]{1,2,0:T(8,128)S(1)}, u32[]{:S(2)}, u32[]{:S(2)}) collective-permute-start(f32[1,128,128]{1,2,0:T(8,128)S(1)} %slice_bitcast_fusion.18), channel_id=1, source_target_pairs={{0,4},{4,8},{8,12},{12,16},{16,20},{20,24},{24,28},{1,5},{5,9},{9,... | collective-permute-start | bytes 196616 | tf_op jit(solution)/shard_map/ppermute | solution.py:16
  114.9 4.3 collective-permute-start.13
  116.2 6.1 %collective-permute-start.14 = (f32[1,128,128]{1,2,0:T(8,128)}, f32[1,128,128]{1,2,0:T(8,128)}, u32[]{:S(2)}, u32[]{:S(2)}) collective-permute-start(f32[1,128,128]{1,2,0:T(8,128)} %get-tuple-element.631), channel_id=1, source_target_pairs={{0,1},{1,2},{2,3},{3,0},{4,5},{5,6},{6,7},{7,4},{8,9},{9,10},{10,1... | collective-permute-start | bytes 196616 | tf_op jit(solution)/shard_map/ppermute | solution.py:16
  116.2 7.4 %collective-permute-start.15 = (f32[1,128,128]{1,2,0:T(8,128)}, f32[1,128,128]{1,2,0:T(8,128)}, u32[]{:S(2)}, u32[]{:S(2)}) collective-permute-start(f32[1,128,128]{1,2,0:T(8,128)} %get-tuple-element.630), channel_id=1, source_target_pairs={{1,0},{2,1},{3,2},{0,3},{5,4},{6,5},{7,6},{4,7},{9,8},{10,9},{11,1... | collective-permute-start | bytes 196616 | tf_op jit(solution)/shard_map/ppermute | solution.py:19
  126.2 1.8 copy-start.4
  170.2 0.6 copy-start.30
  171.9 0.7 copy-start.14
  210.3 3.1 collective-permute-start.16
  213.4 4.3 collective-permute-start.17
  214.7 5.8 %collective-permute-start.18 = (f32[1,128,128]{1,2,0:T(8,128)S(1)}, f32[1,128,128]{1,2,0:T(8,128)S(1)}, u32[]{:S(2)}, u32[]{:S(2)}) collective-permute-start(f32[1,128,128]{1,2,0:T(8,128)S(1)} %get-tuple-element.624), channel_id=1, source_target_pairs={{0,1},{1,2},{2,3},{3,0},{4,5},{5,6},{6,7},{7,4},{8,9},{9,10},{10,1... | collective-permute-start | bytes 196616 | tf_op jit(solution)/shard_map/ppermute | solution.py:16
  214.8 6.4 %collective-permute-start.19 = (f32[1,128,128]{1,2,0:T(8,128)S(1)}, f32[1,128,128]{1,2,0:T(8,128)S(1)}, u32[]{:S(2)}, u32[]{:S(2)}) collective-permute-start(f32[1,128,128]{1,2,0:T(8,128)S(1)} %get-tuple-element.623), channel_id=1, source_target_pairs={{1,0},{2,1},{3,2},{0,3},{5,4},{6,5},{7,6},{4,7},{9,8},{10,9},{11,1... | collective-permute-start | bytes 196616 | tf_op jit(solution)/shard_map/ppermute | solution.py:19
  224.7 42.5 %copy-start.5 = (f32[512,128]{0,1:T(8,128)S(1)}, f32[512,128]{0,1:T(8,128)}, u32[]{:S(2)}) copy-start(f32[512,128]{0,1:T(8,128)} %copy-done.3) | copy-start | bytes 786436
  225.8 41.3 %copy-start.31 = (f32[128]{0:T(128)S(1)}, f32[128]{0:T(128)}, u32[]{:S(2)}) copy-start(f32[128]{0:T(128)} %copy-done.30) | copy-start | bytes 1540
  267.1 69.5 %copy-start.28 = (f32[128]{0:T(128)}, f32[128]{0:T(128)S(1)}, u32[]{:S(2)}) copy-start(f32[128]{0:T(128)S(1)} %psum.67) | copy-start | bytes 1540
  268.2 1.8 copy-start.7
  268.2 1.2 copy-start.18
  275.9 2.2 collective-permute-start.20
  278.7 5.5 %collective-permute-start.21 = (f32[1,128,128]{1,2,0:T(8,128)}, f32[1,128,128]{1,2,0:T(8,128)}, u32[]{:S(2)}, u32[]{:S(2)}) collective-permute-start(f32[1,128,128]{1,2,0:T(8,128)} %get-tuple-element.615), channel_id=1, source_target_pairs={{4,0},{8,4},{12,8},{16,12},{20,16},{24,20},{28,24},{5,1},{9,5},{13... | collective-permute-start | bytes 196616 | tf_op jit(solution)/shard_map/ppermute | solution.py:19
  280.0 5.5 %collective-permute-start.22 = (f32[1,128,128]{1,2,0:T(8,128)}, f32[1,128,128]{1,2,0:T(8,128)}, u32[]{:S(2)}, u32[]{:S(2)}) collective-permute-start(f32[1,128,128]{1,2,0:T(8,128)} %get-tuple-element.617), channel_id=1, source_target_pairs={{0,1},{1,2},{2,3},{3,0},{4,5},{5,6},{6,7},{7,4},{8,9},{9,10},{10,1... | collective-permute-start | bytes 196616 | tf_op jit(solution)/shard_map/ppermute | solution.py:16
  282.3 4.7 collective-permute-start.23
  289.6 1.8 copy-start.8
  337.8 0.7 copy-start.11
  364.9 5.4 %copy-start.27 = (f32[1,8,8]{2,1,0:T(8,128)S(1)}, f32[1,8,8]{2,1,0:T(8,128)}, u32[]{:S(2)}) copy-start(f32[1,8,8]{2,1,0:T(8,128)} %param.33) | copy-start | bytes 772
  376.1 3.1 collective-permute-start.24
  379.2 4.3 collective-permute-start.25
  380.5 5.7 %collective-permute-start.26 = (f32[1,128,128]{1,2,0:T(8,128)S(1)}, f32[1,128,128]{1,2,0:T(8,128)S(1)}, u32[]{:S(2)}, u32[]{:S(2)}) collective-permute-start(f32[1,128,128]{1,2,0:T(8,128)S(1)} %get-tuple-element.610), channel_id=1, source_target_pairs={{0,1},{1,2},{2,3},{3,0},{4,5},{5,6},{6,7},{7,4},{8,9},{9,10},{10,1... | collective-permute-start | bytes 196616 | tf_op jit(solution)/shard_map/ppermute | solution.py:16
  380.6 6.2 %collective-permute-start.27 = (f32[1,128,128]{1,2,0:T(8,128)S(1)}, f32[1,128,128]{1,2,0:T(8,128)S(1)}, u32[]{:S(2)}, u32[]{:S(2)}) collective-permute-start(f32[1,128,128]{1,2,0:T(8,128)S(1)} %get-tuple-element.609), channel_id=1, source_target_pairs={{1,0},{2,1},{3,2},{0,3},{5,4},{6,5},{7,6},{4,7},{9,8},{10,9},{11,1... | collective-permute-start | bytes 196616 | tf_op jit(solution)/shard_map/ppermute | solution.py:19
  390.4 42.9 %copy-start.9 = (f32[128,512]{1,0:T(8,128)S(1)}, f32[128,512]{1,0:T(8,128)}, u32[]{:S(2)}) copy-start(f32[128,512]{1,0:T(8,128)} %copy-done.7) | copy-start | bytes 786436
  391.5 41.7 %copy-start.29 = (f32[128]{0:T(128)S(1)}, f32[128]{0:T(128)}, u32[]{:S(2)}) copy-start(f32[128]{0:T(128)} %copy-done.28) | copy-start | bytes 1540
  434.3 1.8 copy-start.15
  434.3 1.2 copy-start.19
  438.8 2.2 collective-permute-start.28
  441.0 5.3 %collective-permute-start.29 = (f32[1,128,128]{1,2,0:T(8,128)S(1)}, f32[1,128,128]{1,2,0:T(8,128)S(1)}, u32[]{:S(2)}, u32[]{:S(2)}) collective-permute-start(f32[1,128,128]{1,2,0:T(8,128)S(1)} %get-tuple-element.601), channel_id=1, source_target_pairs={{4,0},{8,4},{12,8},{16,12},{20,16},{24,20},{28,24},{5,1},{9,5},{13... | collective-permute-start | bytes 196616 | tf_op jit(solution)/shard_map/ppermute | solution.py:19
  442.3 5.2 %collective-permute-start.30 = (f32[1,128,128]{1,2,0:T(8,128)S(1)}, f32[1,128,128]{1,2,0:T(8,128)S(1)}, u32[]{:S(2)}, u32[]{:S(2)}) collective-permute-start(f32[1,128,128]{1,2,0:T(8,128)S(1)} %get-tuple-element.603), channel_id=1, source_target_pairs={{0,1},{1,2},{2,3},{3,0},{4,5},{5,6},{6,7},{7,4},{8,9},{9,10},{10,1... | collective-permute-start | bytes 196616 | tf_op jit(solution)/shard_map/ppermute | solution.py:16
  444.6 4.4 collective-permute-start.31
  450.1 1.0 copy-start.16
  450.1 45.3 %copy-start.12 = (f32[128,512]{1,0:T(8,128)S(1)}, f32[128,512]{1,0:T(8,128)}, u32[]{:S(2)}) copy-start(f32[128,512]{1,0:T(8,128)} %copy-done.11) | copy-start | bytes 786436
  451.1 44.3 %copy-start.6 = (f32[512,128]{0,1:T(8,128)S(1)}, f32[512,128]{0,1:T(8,128)}, u32[]{:S(2)}) copy-start(f32[512,128]{0,1:T(8,128)} %copy-done.3) | copy-start | bytes 786436
  451.1 44.3 %copy-start.10 = (f32[128,512]{1,0:T(8,128)S(1)}, f32[128,512]{1,0:T(8,128)}, u32[]{:S(2)}) copy-start(f32[128,512]{1,0:T(8,128)} %copy-done.7) | copy-start | bytes 786436
where the time goes:
time: 498 us; the launch traced here: 496 us
  blocking collectives  306 us (61%)
  starting transfers between devices  55.1 us (11%)
  local copies, waits for them, and re-layouts  50 us (10%)
  other arithmetic  34.2 us (7%)
  waiting for transfers between devices  31.1 us (6%)
  matrix products  18.2 us (4%)
    psum x5, blocking collectives, inner_product(): return 0.5 * lax.psum(jnp.sum(first * second, axis=1), ('axial', 'circ'))  212 us
    all_gather x3, blocking collectives, top_level(): lax.all_gather(row_total[None], 'axial', axis=0, tiled=True)  42.7 us
    psum x3, blocking collectives, precondition(): row_total = lax.psum(primal, 'circ')  30 us
    ppermute x16, starting transfers between devices, with_halo(): lax.ppermute(lax.slice_in_dim(block, block.shape[dim] - width, None, axis...  28.2 us
    ppermute x16, starting transfers between devices, with_halo(): lax.ppermute(lax.slice_in_dim(block, 0, width, axis=dim), axis, backward)  26.9 us
    gather x15, local copies, waits for them, and re-layouts, assemble(): return jnp.take(summed, order, axis=-1)  22.4 us
    ppermute x16, waiting for transfers between devices, with_halo(): lax.ppermute(lax.slice_in_dim(block, block.shape[dim] - width, None, axis...  20.7 us
    gather x8, local copies, waits for them, and re-layouts, assemble(): shared = jnp.take(values, inverse, axis=-1)  13.2 us
  transfers between devices with their start and end apart: 32, of which 22 were waited for; matrix products, arithmetic and copies ran while one was open for 1% of the time, Pallas kernels for 0%

commit v1 on v0

v1 whole, which is shorter than its diff:
```python
import functools

import jax
import jax.numpy as jnp
from jax import lax
from jax.experimental import pallas as pl
from jax.experimental.pallas import tpu as pltpu
from jax.sharding import PartitionSpec as P

ITERS = 3
F32 = jnp.float32
BF16 = jnp.bfloat16
MESH = pl.DeviceIdType.MESH
NT = (((1,), (1,)), ((), ()))
HALOS = 1 + 2 * ITERS
SUMS = 2 * ITERS + 1


def split(value):
    high = value.astype(BF16)
    return high, (value - high.astype(F32)).astype(BF16)


def dot16(a, b, dims=(((1,), (0,)), ((), ()))):
    return lax.dot_general(a, b, dims, preferred_element_type=F32)


def kernel(
    rows,
    cols,
    load_ref,
    rho_ref,
    diag_ref,
    couple_ref,
    blocks_ref,
    neumann_ref,
    coarse_ref,
    lower_ref,
    upper_ref,
    order_ref,
    lists_ref,
    x_out,
    r_out,
    hout,
    hin,
    tile_out,
    tile_in,
    c_out,
    c_in,
    a_in,
    coef_in,
    perm,
    schur,
    neumann,
    half,
    vbuf,
    share,
    diag,
    mean,
    own_w,
    near_w,
    x,
    r,
    p,
    b,
    totals,
    hs,
    hr,
    ts,
    tr,
    cs,
    cr,
    as_,
    ar,
    fs,
    fr,
):
    k = lax.axis_index("axial")
    c = lax.axis_index("circ")
    width = perm.shape[1]
    block = blocks_ref.shape[-1]
    list_len = lists_ref.shape[-1]

    def circ_peer(d):
        return {"circ": lax.rem(c + d, cols)}

    def axial_peer(d):
        return {"axial": lax.rem(k + d, rows)}

    barrier = pltpu.get_barrier_semaphore()
    for d in range(1, cols):
        pl.semaphore_signal(barrier, inc=1, device_id=circ_peer(d), device_id_type=MESH)
    for d in range(1, rows):
        pl.semaphore_signal(barrier, inc=1, device_id=axial_peer(d), device_id_type=MESH)

    has = (k > 0, k < rows - 1)
    keep = [has[0].astype(F32), has[1].astype(F32)]

    def across(f):
        if f == 0:
            return {"axial": jnp.maximum(k - 1, 0)}
        if f == 1:
            return {"axial": jnp.minimum(k + 1, rows - 1)}
        return {"circ": lax.rem(c + (cols - 1 if f == 2 else 1), cols)}

    def face_copy(out, into, send, recv, t, f):
        return pltpu.make_async_remote_copy(
            src_ref=out.at[t, f],
            dst_ref=into.at[t, f ^ 1],
            send_sem=send.at[t, f],
            recv_sem=recv.at[t, f ^ 1],
            device_id=across(f),
            device_id_type=MESH,
        )

    def guarded(f, action):
        if f < 2:
            pl.when(has[f])(action)
        else:
            action()

    def send_face(args, t, f):
        guarded(f, lambda: face_copy(*args, t, f).start())

    def wait_face(args, t, f):
        guarded(f, lambda: face_copy(*args, t, f ^ 1).wait_recv())

    def done_face(args, t, f):
        guarded(f, lambda: face_copy(*args, t, f).wait_send())

    halo = (hout, hin, hs, hr)
    tiles = (tile_out, tile_in, ts, tr)

    for f in range(2):

        @pl.when(jnp.logical_not(has[f]))
        def _():
            tile_in[0, f] = jnp.zeros(tile_in.shape[2:], F32)
            for t in range(HALOS):
                hin[t, f] = jnp.zeros(hin.shape[2:], F32)

    sub = lax.broadcasted_iota(jnp.int32, (width, width), 0)
    lane = lax.broadcasted_iota(jnp.int32, (width, width), 1)
    list_sub = lax.broadcasted_iota(jnp.int32, (width, list_len), 0)

    def spread(column):
        return jnp.broadcast_to(column, (width, width))

    def pick(f):
        return perm[f].astype(F32)

    for f in range(4):
        span = pl.ds(f * width, width)
        one = (order_ref[0, :, span] - f * width == sub).astype(F32)
        perm[f] = one.astype(BF16)
        rho = jnp.sum(one * rho_ref[0, :, span], axis=1, keepdims=True)
        dia = jnp.sum(one * diag_ref[0, :, span], axis=1, keepdims=True)
        diag[f] = spread(dia)
        share[f] = spread(rho)
        member = []
        for i in range(2):
            named = (lists_ref[0, 0, pl.ds(2 * f + i, 1), :] - f * width == list_sub).astype(F32)
            member.append(jnp.sum(named, axis=1, keepdims=True))
        pair = jnp.where(lane == 0, member[0], jnp.where(lane == 1, member[1], 0.0))
        pair = dot16(one.astype(BF16), pair.astype(BF16)) / list_len
        mean[2 * f] = spread(pair[:, 0:1])
        mean[2 * f + 1] = spread(pair[:, 1:2])
        packed = jnp.where(
            lane == 0, rho, jnp.where(lane == 1, pair[:, 0:1], jnp.where(lane == 2, pair[:, 1:2], 0.0))
        )
        tile_out[0, f] = packed.T[0:8]
        hout[0, f] = lax.dot_general(
            one,
            load_ref[0, 0, :, span],
            NT,
            precision=lax.Precision.HIGHEST,
            preferred_element_type=F32,
        )

    pl.semaphore_wait(barrier, rows + cols - 2)
    for f in (2, 3, 0, 1):
        send_face(tiles, 0, f)
    for f in (2, 3, 0, 1):
        send_face(halo, 0, f)

    small_sub = lax.broadcasted_iota(jnp.int32, (8, 8), 0)
    small_lane = lax.broadcasted_iota(jnp.int32, (8, 8), 1)
    for i, ref in enumerate((lower_ref, upper_ref)):
        column = jnp.sum(jnp.where(small_sub == small_lane, ref[...], 0.0), axis=1, keepdims=True)
        coef_in[k, i] = jnp.broadcast_to(column, (8, width))

    def coef_copy(d):
        return pltpu.make_async_remote_copy(
            src_ref=coef_in.at[k],
            dst_ref=coef_in.at[k],
            send_sem=fs.at[d],
            recv_sem=fr.at[d],
            device_id=axial_peer(d),
            device_id_type=MESH,
        )

    def coef_arrival(d):
        row = lax.rem(k + rows - d, rows)
        return pltpu.make_async_remote_copy(
            src_ref=coef_in.at[row],
            dst_ref=coef_in.at[row],
            send_sem=fs.at[d],
            recv_sem=fr.at[d],
            device_id=axial_peer(d),
            device_id_type=MESH,
        )

    for d in range(1, rows):
        coef_copy(d).start()

    for f in (0, 1, 2, 3):
        wait_face(tiles, 0, f)
        got = jnp.concatenate([tile_in[0, f], jnp.zeros((width - 8, width), F32)], axis=0).T
        mine = share[f]
        theirs = spread(got[:, 0:1])
        both = mine + theirs
        own_share = mine / both
        near_share = theirs / both
        share[f] = own_share
        masked = own_share * keep[f] if f < 2 else own_share
        for i in range(2):
            own_w[2 * f + i] = masked * mean[2 * f + i]
            near_w[2 * f + i] = near_share * spread(got[:, 1 + i : 2 + i])

    def circ_copy(t, n, d):
        return pltpu.make_async_remote_copy(
            src_ref=c_out.at[t, pl.ds(0, n)],
            dst_ref=c_in.at[t, d, pl.ds(0, n)],
            send_sem=cs.at[t, d],
            recv_sem=cr.at[t, d],
            device_id=circ_peer(d),
            device_id_type=MESH,
        )

    def axial_copy(t, n, d, row):
        return pltpu.make_async_remote_copy(
            src_ref=a_in.at[t, row, pl.ds(0, n)],
            dst_ref=a_in.at[t, row, pl.ds(0, n)],
            send_sem=as_.at[t, d],
            recv_sem=ar.at[t, d],
            device_id=axial_peer(d),
            device_id_type=MESH,
        )

    sizes = {}

    def sum_begin(t, n, value):
        sizes[t] = n
        c_out[t, pl.ds(0, n)] = value
        for d in range(1, cols):
            circ_copy(t, n, d).start()

    def sum_middle(t):
        n = sizes[t]
        value = c_out[t, pl.ds(0, n)]
        for d in range(1, cols):
            circ_copy(t, n, d).wait_recv()
            value = value + c_in[t, d, pl.ds(0, n)]
        a_in[t, k, pl.ds(0, n)] = value
        for d in range(1, rows):
            axial_copy(t, n, d, k).start()

    def sum_end(t):
        n = sizes[t]
        for d in range(1, rows):
            axial_copy(t, n, d, lax.rem(k + rows - d, rows)).wait_recv()

    def dot_total(t, start):
        value = a_in[t, 0, pl.ds(start, 1)]
        for m in range(1, rows):
            value = value + a_in[t, m, pl.ds(start, 1)]
        return 0.0 + value

    sub8 = lax.broadcasted_iota(jnp.int32, (8, width), 0)

    def constraint_tiles(field, extra):
        def one(table, index, f):
            return jnp.sum(table[index] * field(f), axis=0, keepdims=True)

        first = []
        for q in range(8):
            value = own_w[q] * field(q // 2)
            if q in (4, 5):
                value = value + near_w[q + 2] * field(3)
            if q in (6, 7):
                value = value + near_w[q - 2] * field(2)
            first.append(jnp.sum(value, axis=0, keepdims=True))
        second = [one(near_w, 2, 1), one(near_w, 3, 1), one(near_w, 0, 0), one(near_w, 1, 0)]
        second = second + [extra] + [jnp.zeros((1, width), F32)] * 3
        return jnp.concatenate(first + second, axis=0)

    def row_totals(t, m):
        value = a_in[t, m, pl.ds(0, 8)]
        if m > 0:
            value = value + jnp.where(sub8 < 2, a_in[t, m - 1, pl.ds(8, 8)], 0.0)
        if m < rows - 1:
            value = value + jnp.where(
                jnp.logical_and(sub8 >= 2, sub8 < 4), a_in[t, m + 1, pl.ds(8, 8)], 0.0
            )
        return value

    sum_begin(0, 16, constraint_tiles(lambda f: hout[0, f], jnp.zeros((1, width), F32)))

    def store_pair(table, f, cut, value):
        high, low = split(value)
        table[f, pl.ds(0, width), cut] = high
        table[f, pl.ds(width, width), cut] = low

    for f in range(4):
        rows_f = pl.ds(f * width, width)
        high, low = split(neumann_ref[0, 0, rows_f, :])
        high = dot16(perm[f], high).astype(BF16)
        low = dot16(perm[f], low).astype(BF16)
        for g in range(4):
            cut = slice(g * width, (g + 1) * width)
            span = pl.ds(g * width, width)
            neumann[f, pl.ds(0, width), span] = dot16(high[:, cut], perm[g], NT).astype(BF16)
            neumann[f, pl.ds(width, width), span] = dot16(low[:, cut], perm[g], NT).astype(BF16)

    sum_middle(0)

    def apply(table, field):
        for f in range(4):
            high, low = split(field(f))
            vbuf[pl.ds(f * width, width), pl.ds(0, width)] = high
            vbuf[pl.ds(f * width, width), pl.ds(width, width)] = low

        def one(f):
            full = dot16(table[f], vbuf[...])
            small = full[:width, width:] + full[width:, :width] + full[width:, width:]
            return full[:width, :width] + small

        return one

    def assembled(t, f):
        value = hout[t, f] + hin[t, f]
        return value * keep[f] if f < 2 else value

    def coarse_value():
        smooth = []
        h = jnp.zeros((8, width), F32)
        for m in range(rows):
            factor = coef_in[m, 0]
            h = factor * h + (1.0 - factor) * totals[m]
            smooth.append(h)
        top = jnp.zeros((8, width), F32)
        mine = jnp.zeros((8, width), F32)
        for m in reversed(range(rows)):
            factor = coef_in[m, 1]
            top = factor * top + (1.0 - factor) * smooth[m]
            mine = mine + jnp.where(k == m, top, 0.0)
        own = totals[k]
        for q in range(8):
            mine = mine + coarse_ref[0, :, pl.ds(q, 1)] * own[q : q + 1]
        return mine

    def precondition(t, s):
        local = apply(neumann, lambda f: share[f] * r[f])
        coarse = coarse_value()
        partial = None
        for f in (2, 3, 0, 1):
            value = local(f)
            for i in range(2):
                q = 2 * f + i
                value = value + mean[q] * coarse[q : q + 1]
            value = share[f] * value
            hout[t, f] = value
            send_face(halo, t, f)
            term = jnp.sum(r[f] * value, axis=0, keepdims=True)
            partial = term if partial is None else partial + term
        sum_begin(s, 8, jnp.broadcast_to(partial, (8, width)))

    for f in (0, 1, 2, 3):
        wait_face(halo, 0, f)
        r[f] = assembled(0, f)
    sum_end(0)
    for d in range(1, rows):
        coef_arrival(d).wait_recv()
    for m in range(rows):
        totals[m] = row_totals(0, m)
    precondition(1, 1)

    for f in range(4):
        span = pl.ds(f * width, width)
        high, low = split(couple_ref[0, 0, span, :])
        half[0, span, :] = dot16(perm[f], high).astype(BF16)
        half[1, span, :] = dot16(perm[f], low).astype(BF16)
    sum_middle(1)
    for n in range(blocks_ref.shape[2]):
        cut = pl.ds(n * block, block)
        ih, il = split(blocks_ref[0, 0, n])
        ch, cl = half[0, :, cut], half[1, :, cut]
        high, low = split(dot16(ch, ih) + (dot16(ch, il) + dot16(cl, ih)))
        half[2, :, cut] = high
        half[3, :, cut] = low
    for f in range(4):
        span = pl.ds(f * width, width)
        eh, el = half[2, span, :], half[3, span, :]
        ch, cl = half[0], half[1]
        value = dot16(eh, ch, NT) + (dot16(eh, cl, NT) + dot16(el, ch, NT))
        store_pair(schur, f, slice(None), value)

    rz = None
    for step in range(ITERS):
        t = 1 + 2 * step
        for f in (0, 1, 2, 3):
            wait_face(halo, t, f)
        back = apply(schur, lambda f: assembled(t, f))
        if step > 0:
            sum_middle(t)
            sum_end(t)
            new = dot_total(t, 0)
            beta = new / rz
        else:
            sum_end(t)
            new = dot_total(t, 0)
            beta = None
        rz = new
        partial = None
        for f in (2, 3, 0, 1):
            z = assembled(t, f)
            value = diag[f] * z - back(f)
            if beta is not None:
                value = value + beta * hout[t - 1, f]
                z = z + beta * p[f]
            p[f] = z
            hout[t + 1, f] = value
            send_face(halo, t + 1, f)
            term = jnp.sum(z * value, axis=0, keepdims=True)
            partial = term if partial is None else partial + term
        last = step + 1 == ITERS
        if last:
            sum_begin(t + 1, 8, jnp.broadcast_to(partial, (8, width)))
        else:
            sum_begin(t + 1, 16, constraint_tiles(lambda f: hout[t + 1, f], partial))
        sum_middle(t + 1)
        for f in (0, 1, 2, 3):
            wait_face(halo, t + 1, f)
        sum_end(t + 1)
        alpha = rz / dot_total(t + 1, 0 if last else 12)
        for f in range(4):
            x[f] = alpha * p[f] if step == 0 else x[f] + alpha * p[f]
            r[f] = r[f] - alpha * assembled(t + 1, f)
        if not last:
            for m in range(rows):
                totals[m] = totals[m] - alpha * row_totals(t + 1, m)
            precondition(t + 2, t + 2)

    for f in range(4):
        span = pl.ds(f * width, width)
        one = pick(f)
        for ref, field in ((x_out, x), (r_out, r)):
            ref[0, 0, :, span] = jnp.dot(
                field[f].T, one, precision=lax.Precision.HIGHEST, preferred_element_type=F32
            )

    for f in range(4):
        done_face(tiles, 0, f)
        for t in range(HALOS):
            done_face(halo, t, f)
    for d in range(1, rows):
        coef_copy(d).wait_send()
    for t in range(SUMS):
        for d in range(1, cols):
            circ_copy(t, sizes[t], d).wait_send()
        for d in range(1, rows):
            axial_copy(t, sizes[t], d, k).wait_send()


def local(rows, cols, *args):
    load = args[0]
    count, points = load.shape[2:]
    width = points // 4
    dma = pltpu.SemaphoreType.DMA
    face = (4, width, width)
    scratch = [
        pltpu.VMEM((HALOS,) + face, F32),
        pltpu.VMEM((HALOS,) + face, F32),
        pltpu.VMEM((1, 4, 8, width), F32),
        pltpu.VMEM((1, 4, 8, width), F32),
        pltpu.VMEM((SUMS, 16, width), F32),
        pltpu.VMEM((SUMS, cols, 16, width), F32),
        pltpu.VMEM((SUMS, rows, 16, width), F32),
        pltpu.VMEM((rows, 2, 8, width), F32),
        pltpu.VMEM(face, BF16),
        pltpu.VMEM((4, 2 * width, points), BF16),
        pltpu.VMEM((4, 2 * width, points), BF16),
        pltpu.VMEM((4, points, args[3].shape[-1]), BF16),
        pltpu.VMEM((points, 2 * width), BF16),
        pltpu.VMEM(face, F32),
        pltpu.VMEM(face, F32),
        pltpu.VMEM((8, width, width), F32),
        pltpu.VMEM((8, width, width), F32),
        pltpu.VMEM((8, width, width), F32),
        pltpu.VMEM(face, F32),
        pltpu.VMEM(face, F32),
        pltpu.VMEM(face, F32),
        pltpu.VMEM(face, F32),
        pltpu.VMEM((rows, 8, width), F32),
        dma((HALOS, 4)),
        dma((HALOS, 4)),
        dma((1, 4)),
        dma((1, 4)),
        dma((SUMS, cols)),
        dma((SUMS, cols)),
        dma((SUMS, rows)),
        dma((SUMS, rows)),
        dma((rows,)),
        dma((rows,)),
    ]
    shape = jax.ShapeDtypeStruct(load.shape, F32)
    return pl.pallas_call(
        functools.partial(kernel, rows, cols),
        out_shape=(shape, shape),
        in_specs=[pl.BlockSpec(memory_space=pltpu.VMEM)] * len(args),
        out_specs=(pl.BlockSpec(memory_space=pltpu.VMEM),) * 2,
        scratch_shapes=scratch,
        compiler_params=pltpu.CompilerParams(
            collective_id=0, has_side_effects=True, vmem_limit_bytes=40 * 2**20
        ),
    )(*args)


def solution(mesh):
    in_specs = (
        P("axial", "circ", None, None),
        P("axial", "circ", None),
        P("axial", "circ", None),
        P("axial", "circ", None, None),
        P("axial", "circ", None, None, None),
        P("axial", "circ", None, None),
        P("axial", None, None),
        P("axial", None),
        P("axial", None),
        P("axial", "circ", None),
        P("axial", "circ", None, None),
    )
    out_specs = (P("axial", "circ", None, None), P("axial", "circ", None, None))
    body = functools.partial(local, mesh.shape["axial"], mesh.shape["circ"])
    return jax.shard_map(body, mesh=mesh, in_specs=in_specs, out_specs=out_specs, check_vma=False)
```

time: 498 us -> 86.2 us (0.17)
  blocking collectives: 306 us -> 0 us
  Pallas kernels: 0 us -> 74.7 us
  starting transfers between devices: 55.1 us -> 0 us
  local copies, waits for them, and re-layouts: 50 us -> 10.5 us
  other arithmetic: 34.2 us -> 0 us
  waiting for transfers between devices: 31.1 us -> 0 us
  matrix products: 18.2 us -> 0 us
    psum x8 -> x0, blocking collectives: 242 us -> none  [the longest x5 212 us: inner_product(): return 0.5 * lax.psum(jnp.sum(first * second, axis=1), ('axial', 'circ'))]
    pallas_call x0 -> x1, Pallas kernels: none -> 74.7 us  [local(): pl.pallas_call(functools.partial(kernel, rows, cols), out_shape=(shape, s...]
    all_gather x5 -> x0, blocking collectives: 64 us -> none  [the longest x3 42.7 us: top_level(): lax.all_gather(row_total[None], 'axial', axis=0, tiled=True)]
    ppermute x32 -> x0, starting transfers between devices: 55.1 us -> none  [the longest x16 28.2 us: with_halo(): lax.ppermute(lax.slice_in_dim(block, block.shape[dim] - width, None, axis...]
    gather x23 -> x0, local copies, waits for them, and re-layouts: 35.6 us -> none  [the longest x15 22.4 us: assemble(): return jnp.take(summed, order, axis=-1)]
    ppermute x32 -> x0, waiting for transfers between devices: 31.1 us -> none  [the longest x16 20.7 us: with_halo(): lax.ppermute(lax.slice_in_dim(block, block.shape[dim] - width, None, axis...]
    dot_general x21 -> x0, matrix products: 18.2 us -> none  [the longest x3 5.23 us: local(): lax.dot_general(solved, couple_local, (((1,), (1,)), ((), ())), precision...]
    dynamic_update_slice x48 -> x0, other arithmetic: 13.1 us -> none  [top_level(): lax.scan(forward_step, start, (all_lower[:, None, :], all_rows))]
  transfers between devices with their start and end apart: 32 -> 0, of which waited for: 22 -> 0; matrix products, arithmetic and copies ran while one was open for 1% -> 0% of each run, Pallas kernels for 0% -> 0%
where the time goes in v1:
time: 86.2 us; the launch traced here: 85.8 us
  Pallas kernels  74.7 us (87%)
  local copies, waits for them, and re-layouts  10.5 us (12%)
    pallas_call x1, Pallas kernels, local(): pl.pallas_call(functools.partial(kernel, rows, cols), out_shape=(shape, s...  74.7 us
    unnamed x24, local copies, waits for them, and re-layouts  10.5 us

profile of v1, /device:TPU:0, one launch (start us, length us, event | category | flops | bytes accessed | tf_op | source)
XLA Modules:
  0.0 85.8 jit_solution(17288344171138511330)
XLA Ops:
  0.6 0.0 copy-start
  0.6 1.2 %copy-done = f32[1,1,512,512]{3,2,1,0:T(8,128)S(1)} copy-done((f32[1,1,512,512]{3,2,1,0:T(8,128)S(1)}, f32[1,1,512,512]{3,2,1,0:T(8,128)}, u32[]{:S(2)}) %copy-start) | copy-done | bytes 1048600
  1.9 0.0 copy-start.1
  1.9 1.2 %copy-done.1 = f32[1,1,512,512]{3,2,1,0:T(8,128)S(1)} copy-done((f32[1,1,512,512]{3,2,1,0:T(8,128)S(1)}, f32[1,1,512,512]{3,2,1,0:T(8,128)}, u32[]{:S(2)}) %copy-start.1) | copy-done | bytes 1048600
  3.1 0.0 copy-start.2
  3.1 0.9 %copy-done.2 = f32[1,1,128,512]{3,2,1,0:T(8,128)S(1)} copy-done((f32[1,1,128,512]{3,2,1,0:T(8,128)S(1)}, f32[1,1,128,512]{3,2,1,0:T(8,128)}, u32[]{:S(2)}) %copy-start.2) | copy-done | bytes 262168
  4.0 0.0 copy-start.3
  4.0 0.9 %copy-done.3 = f32[1,1,4,128,128]{4,3,2,1,0:T(8,128)S(1)} copy-done((f32[1,1,4,128,128]{4,3,2,1,0:T(8,128)S(1)}, f32[1,1,4,128,128]{4,3,2,1,0:T(8,128)}, u32[]{:S(2)}) %copy-start.3) | copy-done | bytes 262168
  5.0 0.0 copy-start.4
  5.0 0.7 copy-done.4
  5.7 0.0 copy-start.5
  5.7 0.7 copy-done.5
  6.4 0.0 copy-start.6
  6.4 0.7 copy-done.6
  7.0 0.0 copy-start.7
  7.0 0.7 copy-done.7
  7.7 0.0 copy-start.8
  7.7 0.7 copy-done.8
  8.4 0.0 copy-start.9
  8.4 0.7 copy-done.9
  9.1 0.0 copy-start.10
  9.1 0.7 copy-done.10
  9.7 74.7 %shard_map.122 = (f32[1,1,128,512]{3,2,1,0:T(8,128)S(1)}, f32[1,1,128,512]{3,2,1,0:T(8,128)S(1)}) custom-call(f32[1,1,128,512]{3,2,1,0:T(8,128)S(1)} %copy-done.2, f32[1,1,512]{2,1,0:T(1,128)S(1)} %copy-done.6, f32[1,1,512]{2,1,0:T(1,128)S(1)} %copy-done.7, f32[1,1,512,512]{3,2,1,0:T(8,128)S(1)} %copy-done, f32[1,1,4,128,128]{4,3,2,1,0:T(8,128)S(1)} %copy-done.3, ...), custom_call_target="tpu_custom_call" | custom-call | tf_op jit(solution)/shard_map/pallas_call | solution.py:517
  84.4 0.7 copy.15
  85.1 0.7 copy.16
Async XLA Ops:
  0.6 1.2 %copy-start = (f32[1,1,512,512]{3,2,1,0:T(8,128)S(1)}, f32[1,1,512,512]{3,2,1,0:T(8,128)}, u32[]{:S(2)}) copy-start(f32[1,1,512,512]{3,2,1,0:T(8,128)} %couple_ref.1) | copy-start | bytes 3145732
  1.9 1.2 %copy-start.1 = (f32[1,1,512,512]{3,2,1,0:T(8,128)S(1)}, f32[1,1,512,512]{3,2,1,0:T(8,128)}, u32[]{:S(2)}) copy-start(f32[1,1,512,512]{3,2,1,0:T(8,128)} %neumann_ref.1) | copy-start | bytes 3145732
  3.1 0.9 %copy-start.2 = (f32[1,1,128,512]{3,2,1,0:T(8,128)S(1)}, f32[1,1,128,512]{3,2,1,0:T(8,128)}, u32[]{:S(2)}) copy-start(f32[1,1,128,512]{3,2,1,0:T(8,128)} %load_ref.1) | copy-start | bytes 786436
  4.0 0.9 %copy-start.3 = (f32[1,1,4,128,128]{4,3,2,1,0:T(8,128)S(1)}, f32[1,1,4,128,128]{4,3,2,1,0:T(8,128)}, u32[]{:S(2)}) copy-start(f32[1,1,4,128,128]{4,3,2,1,0:T(8,128)} %blocks_ref.1) | copy-start | bytes 786436
  5.0 0.7 copy-start.4
  5.7 0.7 copy-start.5
  6.4 0.7 copy-start.6
  7.0 0.7 copy-start.7
  7.7 0.7 copy-start.8
  8.4 0.7 copy-start.9
  9.1 0.7 copy-start.10

commit v2 on v1

--- a/solution.py
+++ b/solution.py
@@ -13,7 +13,7 @@
 MESH = pl.DeviceIdType.MESH
 NT = (((1,), (1,)), ((), ()))
 HALOS = 1 + 2 * ITERS
-SUMS = 2 * ITERS + 1
+SUMS = 1 + ITERS
 
 
 def split(value):
@@ -28,56 +28,29 @@
 def kernel(
     rows,
     cols,
-    load_ref,
-    rho_ref,
-    diag_ref,
-    couple_ref,
-    blocks_ref,
-    neumann_ref,
-    coarse_ref,
-    lower_ref,
-    upper_ref,
-    order_ref,
-    lists_ref,
-    x_out,
-    r_out,
-    hout,
-    hin,
-    tile_out,
-    tile_in,
-    c_out,
-    c_in,
-    a_in,
-    coef_in,
-    perm,
-    schur,
-    neumann,
-    half,
-    vbuf,
-    share,
-    diag,
-    mean,
-    own_w,
-    near_w,
-    x,
-    r,
-    p,
-    b,
-    totals,
-    hs,
-    hr,
-    ts,
-    tr,
-    cs,
-    cr,
-    as_,
-    ar,
-    fs,
-    fr,
+    *refs,
 ):
+    sources, refs = refs[:11], refs[11:]
+    (x_out, r_out), refs = refs[:2], refs[2:]
+    held, in_sem, refs = refs[:11], refs[11], refs[12:]
+    (
+        load_ref, rho_ref, diag_ref, couple_ref, blocks_ref, neumann_ref,
+        coarse_ref, lower_ref, upper_ref, order_ref, lists_ref,
+    ) = held
+    (
+        hout, hin, tile_out, tile_in, c_out, c_in, a_in, coef_in, perm, schur, neumann, half, vbuf,
+        share, diag, mean, own_w, near_w, x, r, p, image, totals, moved,
+        hs, hr, ts, tr, cs, cr, as_, ar, fs, fr,
+    ) = refs
     k = lax.axis_index("axial")
     c = lax.axis_index("circ")
     width = perm.shape[1]
+    arrivals = [
+        pltpu.make_async_copy(source, target, in_sem.at[i])
+        for i, (source, target) in enumerate(zip(sources, held))
+    ]
+    for i in (9, 1, 2, 10, 0, 7, 8, 6, 5, 3, 4):
+        arrivals[i].start()
     block = blocks_ref.shape[-1]
     list_len = lists_ref.shape[-1]
 
@@ -148,6 +121,9 @@
 
     def pick(f):
         return perm[f].astype(F32)
+
+    for i in (9, 1, 2, 10, 0):
+        arrivals[i].wait()
 
     for f in range(4):
         span = pl.ds(f * width, width)
@@ -183,6 +159,9 @@
     for f in (2, 3, 0, 1):
         send_face(halo, 0, f)
 
+    for i in (7, 8, 6):
+        arrivals[i].wait()
+
     small_sub = lax.broadcasted_iota(jnp.int32, (8, 8), 0)
     small_lane = lax.broadcasted_iota(jnp.int32, (8, 8), 1)
     for i, ref in enumerate((lower_ref, upper_ref)):
@@ -227,58 +206,60 @@
             own_w[2 * f + i] = masked * mean[2 * f + i]
             near_w[2 * f + i] = near_share * spread(got[:, 1 + i : 2 + i])
 
-    def circ_copy(t, n, d):
+    def span_of(t):
+        return pl.ds(8, 8) if t == ITERS else pl.ds(0, 16)
+
+    def circ_copy(t, d):
         return pltpu.make_async_remote_copy(
-            src_ref=c_out.at[t, pl.ds(0, n)],
-            dst_ref=c_in.at[t, d, pl.ds(0, n)],
+            src_ref=c_out.at[t, span_of(t)],
+            dst_ref=c_in.at[t, d, span_of(t)],
             send_sem=cs.at[t, d],
             recv_sem=cr.at[t, d],
             device_id=circ_peer(d),
             device_id_type=MESH,
         )
 
-    def axial_copy(t, n, d, row):
+    def axial_copy(t, d, row):
         return pltpu.make_async_remote_copy(
-            src_ref=a_in.at[t, row, pl.ds(0, n)],
-            dst_ref=a_in.at[t, row, pl.ds(0, n)],
+            src_ref=a_in.at[t, row, span_of(t)],
+            dst_ref=a_in.at[t, row, span_of(t)],
             send_sem=as_.at[t, d],
             recv_sem=ar.at[t, d],
             device_id=axial_peer(d),
             device_id_type=MESH,
         )
 
-    sizes = {}
-
-    def sum_begin(t, n, value):
-        sizes[t] = n
-        c_out[t, pl.ds(0, n)] = value
+    def sum_begin(t, value):
+        c_out[t, span_of(t)] = value
         for d in range(1, cols):
-            circ_copy(t, n, d).start()
+            circ_copy(t, d).start()
 
     def sum_middle(t):
-        n = sizes[t]
-        value = c_out[t, pl.ds(0, n)]
+        value = c_out[t, span_of(t)]
         for d in range(1, cols):
-            circ_copy(t, n, d).wait_recv()
-            value = value + c_in[t, d, pl.ds(0, n)]
-        a_in[t, k, pl.ds(0, n)] = value
+            circ_copy(t, d).wait_recv()
+            value = value + c_in[t, d, span_of(t)]
+        a_in[t, k, span_of(t)] = value
         for d in range(1, rows):
-            axial_copy(t, n, d, k).start()
+            axial_copy(t, d, k).start()
 
     def sum_end(t):
-        n = sizes[t]
         for d in range(1, rows):
-            axial_copy(t, n, d, lax.rem(k + rows - d, rows)).wait_recv()
-
-    def dot_total(t, start):
-        value = a_in[t, 0, pl.ds(start, 1)]
+            axial_copy(t, d, lax.rem(k + rows - d, rows)).wait_recv()
+
+    def dot_total(t, row):
+        value = a_in[t, 0, pl.ds(row, 1)]
         for m in range(1, rows):
-            value = value + a_in[t, m, pl.ds(start, 1)]
-        return 0.0 + value
+            value = value + a_in[t, m, pl.ds(row, 1)]
+        return value
 
     sub8 = lax.broadcasted_iota(jnp.int32, (8, width), 0)
 
-    def constraint_tiles(field, extra):
+    def dot_tile(dots, head):
+        dots = dots + [jnp.zeros((1, width), F32)] * (4 - len(dots))
+        return jnp.concatenate(head + dots, axis=0)
+
+    def constraint_tiles(field, dots):
         def one(table, index, f):
             return jnp.sum(table[index] * field(f), axis=0, keepdims=True)
 
@@ -291,8 +272,7 @@
                 value = value + near_w[q - 2] * field(2)
             first.append(jnp.sum(value, axis=0, keepdims=True))
         second = [one(near_w, 2, 1), one(near_w, 3, 1), one(near_w, 0, 0), one(near_w, 1, 0)]
-        second = second + [extra] + [jnp.zeros((1, width), F32)] * 3
-        return jnp.concatenate(first + second, axis=0)
+        return dot_tile(dots, first + second)
 
     def row_totals(t, m):
         value = a_in[t, m, pl.ds(0, 8)]
@@ -304,7 +284,9 @@
             )
         return value
 
-    sum_begin(0, 16, constraint_tiles(lambda f: hout[0, f], jnp.zeros((1, width), F32)))
+    sum_begin(0, constraint_tiles(lambda f: hout[0, f], []))
+
+    arrivals[5].wait()
 
     def store_pair(table, f, cut, value):
         high, low = split(value)
@@ -359,10 +341,9 @@
             mine = mine + coarse_ref[0, :, pl.ds(q, 1)] * own[q : q + 1]
         return mine
 
-    def precondition(t, s):
+    def precondition(t):
         local = apply(neumann, lambda f: share[f] * r[f])
         coarse = coarse_value()
-        partial = None
         for f in (2, 3, 0, 1):
             value = local(f)
             for i in range(2):
@@ -371,9 +352,6 @@
             value = share[f] * value
             hout[t, f] = value
             send_face(halo, t, f)
-            term = jnp.sum(r[f] * value, axis=0, keepdims=True)
-            partial = term if partial is None else partial + term
-        sum_begin(s, 8, jnp.broadcast_to(partial, (8, width)))
 
     for f in (0, 1, 2, 3):
         wait_face(halo, 0, f)
@@ -383,14 +361,16 @@
         coef_arrival(d).wait_recv()
     for m in range(rows):
         totals[m] = row_totals(0, m)
-    precondition(1, 1)
+    precondition(1)
+
+    arrivals[3].wait()
+    arrivals[4].wait()
 
     for f in range(4):
         span = pl.ds(f * width, width)
         high, low = split(couple_ref[0, 0, span, :])
         half[0, span, :] = dot16(perm[f], high).astype(BF16)
         half[1, span, :] = dot16(perm[f], low).astype(BF16)
-    sum_middle(1)
     for n in range(blocks_ref.shape[2]):
         cut = pl.ds(n * block, block)
         ih, il = split(blocks_ref[0, 0, n])
@@ -405,51 +385,61 @@
         value = dot16(eh, ch, NT) + (dot16(eh, cl, NT) + dot16(el, ch, NT))
         store_pair(schur, f, slice(None), value)
 
+    def fold(value):
+        return jnp.sum(value, axis=0, keepdims=True)
+
     rz = None
+    pap = None
     for step in range(ITERS):
         t = 1 + 2 * step
+        last = step + 1 == ITERS
         for f in (0, 1, 2, 3):
             wait_face(halo, t, f)
         back = apply(schur, lambda f: assembled(t, f))
-        if step > 0:
-            sum_middle(t)
-            sum_end(t)
-            new = dot_total(t, 0)
-            beta = new / rz
-        else:
-            sum_end(t)
-            new = dot_total(t, 0)
-            beta = None
-        rz = new
-        partial = None
+        dots = [jnp.zeros((1, width), F32) for _ in range(2 if step == 0 else 3)]
         for f in (2, 3, 0, 1):
             z = assembled(t, f)
             value = diag[f] * z - back(f)
-            if beta is not None:
-                value = value + beta * hout[t - 1, f]
-                z = z + beta * p[f]
-            p[f] = z
             hout[t + 1, f] = value
+            dots[0] = dots[0] + 0.5 * fold(r[f] * z)
+            dots[1] = dots[1] + fold(z * value)
+            if step > 0:
+                dots[2] = dots[2] + fold(0.5 * (z * image[f]) + p[f] * value)
+        if last:
+            sum_begin(step + 1, dot_tile(dots, [jnp.zeros((1, width), F32)] * 4))
+        else:
+            sum_begin(step + 1, constraint_tiles(lambda f: hout[t + 1, f], dots))
+        for f in (2, 3, 0, 1):
             send_face(halo, t + 1, f)
-            term = jnp.sum(z * value, axis=0, keepdims=True)
-            partial = term if partial is None else partial + term
-        last = step + 1 == ITERS
-        if last:
-            sum_begin(t + 1, 8, jnp.broadcast_to(partial, (8, width)))
-        else:
-            sum_begin(t + 1, 16, constraint_tiles(lambda f: hout[t + 1, f], partial))
-        sum_middle(t + 1)
+        sum_middle(step + 1)
         for f in (0, 1, 2, 3):
             wait_face(halo, t + 1, f)
-        sum_end(t + 1)
-        alpha = rz / dot_total(t + 1, 0 if last else 12)
+        sum_end(step + 1)
+        new = dot_total(step + 1, 12)
+        new_pap = dot_total(step + 1, 13)
+        if step > 0:
+            beta = new / rz
+            new_pap = new_pap + beta * (dot_total(step + 1, 14) + beta * pap)
+        rz, pap = new, new_pap
+        alpha = rz / pap
         for f in range(4):
-            x[f] = alpha * p[f] if step == 0 else x[f] + alpha * p[f]
-            r[f] = r[f] - alpha * assembled(t + 1, f)
+            z = assembled(t, f)
+            w = assembled(t + 1, f)
+            if step > 0:
+                z = z + beta * p[f]
+                w = w + beta * image[f]
+            p[f] = z
+            image[f] = w
+            x[f] = alpha * z if step == 0 else x[f] + alpha * z
+            r[f] = r[f] - alpha * w
         if not last:
             for m in range(rows):
-                totals[m] = totals[m] - alpha * row_totals(t + 1, m)
-            precondition(t + 2, t + 2)
+                value = row_totals(step + 1, m)
+                if step > 0:
+                    value = value + beta * moved[m]
+                moved[m] = value
+                totals[m] = totals[m] - alpha * value
+            precondition(t + 2)
 
     for f in range(4):
         span = pl.ds(f * width, width)
@@ -467,9 +457,9 @@
         coef_copy(d).wait_send()
     for t in range(SUMS):
         for d in range(1, cols):
-            circ_copy(t, sizes[t], d).wait_send()
+            circ_copy(t, d).wait_send()
         for d in range(1, rows):
-            axial_copy(t, sizes[t], d, k).wait_send()
+            axial_copy(t, d, k).wait_send()
 
 
 def local(rows, cols, *args):
@@ -478,7 +468,8 @@
     width = points // 4
     dma = pltpu.SemaphoreType.DMA
     face = (4, width, width)
-    scratch = [
+    scratch = [pltpu.VMEM(arg.shape, arg.dtype) for arg in args] + [
+        dma((len(args),)),
         pltpu.VMEM((HALOS,) + face, F32),
         pltpu.VMEM((HALOS,) + face, F32),
         pltpu.VMEM((1, 4, 8, width), F32),
@@ -502,6 +493,7 @@
         pltpu.VMEM(face, F32),
         pltpu.VMEM(face, F32),
         pltpu.VMEM((rows, 8, width), F32),
+        pltpu.VMEM((rows, 8, width), F32),
         dma((HALOS, 4)),
         dma((HALOS, 4)),
         dma((1, 4)),
@@ -517,11 +509,11 @@
     return pl.pallas_call(
         functools.partial(kernel, rows, cols),
         out_shape=(shape, shape),
-        in_specs=[pl.BlockSpec(memory_space=pltpu.VMEM)] * len(args),
+        in_specs=[pl.BlockSpec(memory_space=pl.ANY)] * len(args),
         out_specs=(pl.BlockSpec(memory_space=pltpu.VMEM),) * 2,
         scratch_shapes=scratch,
         compiler_params=pltpu.CompilerParams(
-            collective_id=0, has_side_effects=True, vmem_limit_bytes=40 * 2**20
+            collective_id=0, has_side_effects=True, vmem_limit_bytes=56 * 2**20
         ),
     )(*args)
 

time: 86.2 us -> 61.4 us (0.71)
  Pallas kernels: 74.7 us -> 58.2 us
  local copies, waits for them, and re-layouts: 10.5 us -> 2.42 us
    pallas_call x1, Pallas kernels: 74.7 us -> 58.2 us  [local(): pl.pallas_call(functools.partial(kernel, rows, cols), out_shape=(shape, s...]
    unnamed x24 -> x4, local copies, waits for them, and re-layouts: 10.5 us -> 2.42 us
where the time goes in v2:
time: 61.4 us; the launch traced here: 61.2 us
  Pallas kernels  58.2 us (95%)
  local copies, waits for them, and re-layouts  2.42 us (4%)
  between operations  0.65 us (1%)
    pallas_call x1, Pallas kernels, local(): pl.pallas_call(functools.partial(kernel, rows, cols), out_shape=(shape, s...  58.2 us
    unnamed x4, local copies, waits for them, and re-layouts  2.42 us

profile of v2, /device:TPU:0, one launch (start us, length us, event | category | flops | bytes accessed | tf_op | source)
XLA Modules:
  0.0 61.2 jit_solution(2756986455948927853)
XLA Ops:
  0.6 58.2 %shard_map.122 = (f32[1,1,128,512]{3,2,1,0:T(8,128)}, f32[1,1,128,512]{3,2,1,0:T(8,128)}) custom-call(f32[1,1,128,512]{3,2,1,0:T(8,128)} %refs_0_.1, f32[1,1,512]{2,1,0:T(1,128)} %refs_1_.1, f32[1,1,512]{2,1,0:T(1,128)} %refs_2_.1, f32[1,1,512,512]{3,2,1,0:T(8,128)} %refs_3_.1, f32[1,1,4,128,128]{4,3,2,1,0:T(8,128)} %refs_4_.1, f32[1,1,512,512]{3,2,1,0:T(8,128)} %refs_5_.1, ...), custom_call_target="tpu_custom_call" | custom-call | tf_op jit(solution)/shard_map/pallas_call | solution.py:509
  58.8 0.0 copy-start
  58.8 1.7 %copy.15 = f32[1,1,128,512]{3,2,1,0:T(8,128)} copy(f32[1,1,128,512]{3,2,1,0:T(8,128)} %get-tuple-element.4) | data formatting | bytes 524288
  60.5 0.0 copy-done
  60.5 0.7 %copy.16 = f32[1,1,128,512]{3,2,1,0:T(8,128)} copy(f32[1,1,128,512]{3,2,1,0:T(8,128)S(1)} %copy-done) | data formatting | bytes 524288
Async XLA Ops:
  58.8 1.7 %copy-start = (f32[1,1,128,512]{3,2,1,0:T(8,128)S(1)}, f32[1,1,128,512]{3,2,1,0:T(8,128)}, u32[]{:S(2)}) copy-start(f32[1,1,128,512]{3,2,1,0:T(8,128)} %get-tuple-element.5) | copy-start | bytes 786436

commit v3 on v2

--- a/solution.py
+++ b/solution.py
@@ -14,6 +14,7 @@
 NT = (((1,), (1,)), ((), ()))
 HALOS = 1 + 2 * ITERS
 SUMS = 1 + ITERS
+GROUPS = 2
 
 
 def split(value):
@@ -45,6 +46,7 @@
     k = lax.axis_index("axial")
     c = lax.axis_index("circ")
     width = perm.shape[1]
+    fold_rows = width // GROUPS
     arrivals = [
         pltpu.make_async_copy(source, target, in_sem.at[i])
         for i, (source, target) in enumerate(zip(sources, held))
@@ -109,15 +111,23 @@
         @pl.when(jnp.logical_not(has[f]))
         def _():
             tile_in[0, f] = jnp.zeros(tile_in.shape[2:], F32)
-            for t in range(HALOS):
+            for t in range(GROUPS * HALOS):
                 hin[t, f] = jnp.zeros(hin.shape[2:], F32)
 
     sub = lax.broadcasted_iota(jnp.int32, (width, width), 0)
     lane = lax.broadcasted_iota(jnp.int32, (width, width), 1)
     list_sub = lax.broadcasted_iota(jnp.int32, (width, list_len), 0)
 
+    low_lanes = lane[:fold_rows] < fold_rows
+    low8 = lane[:8] < fold_rows
+
+    def roll(value):
+        return pltpu.roll(value, fold_rows, 1)
+
     def spread(column):
-        return jnp.broadcast_to(column, (width, width))
+        shape = (fold_rows, width)
+        first = jnp.broadcast_to(column[:fold_rows], shape)
+        return jnp.where(low_lanes, first, jnp.broadcast_to(column[fold_rows:], shape))
 
     def pick(f):
         return perm[f].astype(F32)
@@ -145,19 +155,23 @@
             lane == 0, rho, jnp.where(lane == 1, pair[:, 0:1], jnp.where(lane == 2, pair[:, 1:2], 0.0))
         )
         tile_out[0, f] = packed.T[0:8]
-        hout[0, f] = lax.dot_general(
+        whole = lax.dot_general(
             one,
             load_ref[0, 0, :, span],
             NT,
             precision=lax.Precision.HIGHEST,
             preferred_element_type=F32,
         )
+        top, bottom = whole[:fold_rows], whole[fold_rows:]
+        hout[0, f] = jnp.where(low_lanes, top, roll(bottom))
+        hout[1, f] = jnp.where(low_lanes, roll(top), bottom)
 
     pl.semaphore_wait(barrier, rows + cols - 2)
     for f in (2, 3, 0, 1):
         send_face(tiles, 0, f)
-    for f in (2, 3, 0, 1):
-        send_face(halo, 0, f)
+    for g in range(GROUPS):
+        for f in (2, 3, 0, 1):
+            send_face(halo, g, f)
 
     for i in (7, 8, 6):
         arrivals[i].wait()
@@ -206,13 +220,10 @@
             own_w[2 * f + i] = masked * mean[2 * f + i]
             near_w[2 * f + i] = near_share * spread(got[:, 1 + i : 2 + i])
 
-    def span_of(t):
-        return pl.ds(8, 8) if t == ITERS else pl.ds(0, 16)
-
     def circ_copy(t, d):
         return pltpu.make_async_remote_copy(
-            src_ref=c_out.at[t, span_of(t)],
-            dst_ref=c_in.at[t, d, span_of(t)],
+            src_ref=c_out.at[t],
+            dst_ref=c_in.at[t, d],
             send_sem=cs.at[t, d],
             recv_sem=cr.at[t, d],
             device_id=circ_peer(d),
@@ -221,8 +232,8 @@
 
     def axial_copy(t, d, row):
         return pltpu.make_async_remote_copy(
-            src_ref=a_in.at[t, row, span_of(t)],
-            dst_ref=a_in.at[t, row, span_of(t)],
+            src_ref=a_in.at[t, row],
+            dst_ref=a_in.at[t, row],
             send_sem=as_.at[t, d],
             recv_sem=ar.at[t, d],
             device_id=axial_peer(d),
@@ -230,16 +241,16 @@
         )
 
     def sum_begin(t, value):
-        c_out[t, span_of(t)] = value
+        c_out[t] = value
         for d in range(1, cols):
             circ_copy(t, d).start()
 
     def sum_middle(t):
-        value = c_out[t, span_of(t)]
+        value = c_out[t]
         for d in range(1, cols):
             circ_copy(t, d).wait_recv()
-            value = value + c_in[t, d, span_of(t)]
-        a_in[t, k, span_of(t)] = value
+            value = value + c_in[t, d]
+        a_in[t, k] = value
         for d in range(1, rows):
             axial_copy(t, d, k).start()
 
@@ -251,18 +262,23 @@
         value = a_in[t, 0, pl.ds(row, 1)]
         for m in range(1, rows):
             value = value + a_in[t, m, pl.ds(row, 1)]
-        return value
+        return jnp.where(low8[:1], roll(value), value)
 
     sub8 = lax.broadcasted_iota(jnp.int32, (8, width), 0)
 
-    def dot_tile(dots, head):
-        dots = dots + [jnp.zeros((1, width), F32)] * (4 - len(dots))
-        return jnp.concatenate(head + dots, axis=0)
-
-    def constraint_tiles(field, dots):
-        def one(table, index, f):
-            return jnp.sum(table[index] * field(f), axis=0, keepdims=True)
-
+    def packed_tile(first, second):
+        zero = jnp.zeros((1, width), F32)
+        second = jnp.concatenate(second + [zero] * (8 - len(second)), axis=0)
+        second = second + roll(second)
+        if first is None:
+            return second
+        first = jnp.concatenate(first, axis=0)
+        return jnp.where(low8, first + roll(first), second)
+
+    def fold(value):
+        return jnp.sum(value, axis=0, keepdims=True)
+
+    def constraint_tile(field, dots):
         first = []
         for q in range(8):
             value = own_w[q] * field(q // 2)
@@ -270,21 +286,25 @@
                 value = value + near_w[q + 2] * field(3)
             if q in (6, 7):
                 value = value + near_w[q - 2] * field(2)
-            first.append(jnp.sum(value, axis=0, keepdims=True))
-        second = [one(near_w, 2, 1), one(near_w, 3, 1), one(near_w, 0, 0), one(near_w, 1, 0)]
-        return dot_tile(dots, first + second)
+            first.append(fold(value))
+        second = [fold(near_w[i] * field(i // 2)) for i in (2, 3, 0, 1)]
+        return packed_tile(first, second + dots)
 
     def row_totals(t, m):
-        value = a_in[t, m, pl.ds(0, 8)]
+        value = a_in[t, m]
+        value = jnp.where(low8, value, roll(value))
         if m > 0:
-            value = value + jnp.where(sub8 < 2, a_in[t, m - 1, pl.ds(8, 8)], 0.0)
+            other = a_in[t, m - 1]
+            other = jnp.where(low8, roll(other), other)
+            value = value + jnp.where(sub8 < 2, other, 0.0)
         if m < rows - 1:
-            value = value + jnp.where(
-                jnp.logical_and(sub8 >= 2, sub8 < 4), a_in[t, m + 1, pl.ds(8, 8)], 0.0
-            )
+            other = a_in[t, m + 1]
+            other = jnp.where(low8, roll(other), other)
+            value = value + jnp.where(jnp.logical_and(sub8 >= 2, sub8 < 4), other, 0.0)
         return value
 
-    sum_begin(0, constraint_tiles(lambda f: hout[0, f], []))
+    for g in range(GROUPS):
+        sum_begin(g, constraint_tile(lambda f: hout[g, f], []))
 
     arrivals[5].wait()
 
@@ -304,18 +324,24 @@
             neumann[f, pl.ds(0, width), span] = dot16(high[:, cut], perm[g], NT).astype(BF16)
             neumann[f, pl.ds(width, width), span] = dot16(low[:, cut], perm[g], NT).astype(BF16)
 
-    sum_middle(0)
-
-    def apply(table, field):
+    for g in range(GROUPS):
+        sum_middle(g)
+
+    def apply(table, g, field):
         for f in range(4):
-            high, low = split(field(f))
-            vbuf[pl.ds(f * width, width), pl.ds(0, width)] = high
-            vbuf[pl.ds(f * width, width), pl.ds(width, width)] = low
+            value = field(f)
+            high = value.astype(BF16).astype(F32)
+            low = value - high
+            top = jnp.where(low_lanes, high, roll(low))
+            bottom = jnp.where(low_lanes, roll(high), low)
+            vbuf[g, pl.ds(f * width, fold_rows), :] = top.astype(BF16)
+            vbuf[g, pl.ds(f * width + fold_rows, fold_rows), :] = bottom.astype(BF16)
 
         def one(f):
-            full = dot16(table[f], vbuf[...])
-            small = full[:width, width:] + full[width:, :width] + full[width:, width:]
-            return full[:width, :width] + small
+            full = dot16(table[f], vbuf[g])
+            full = full[:width] + full[width:]
+            top, bottom = full[:fold_rows], full[fold_rows:]
+            return jnp.where(low_lanes, top, bottom) + roll(jnp.where(low_lanes, bottom, top))
 
         return one
 
@@ -323,12 +349,12 @@
         value = hout[t, f] + hin[t, f]
         return value * keep[f] if f < 2 else value
 
-    def coarse_value():
+    def coarse_value(g):
         smooth = []
         h = jnp.zeros((8, width), F32)
         for m in range(rows):
             factor = coef_in[m, 0]
-            h = factor * h + (1.0 - factor) * totals[m]
+            h = factor * h + (1.0 - factor) * totals[g, m]
             smooth.append(h)
         top = jnp.zeros((8, width), F32)
         mine = jnp.zeros((8, width), F32)
@@ -336,32 +362,34 @@
             factor = coef_in[m, 1]
             top = factor * top + (1.0 - factor) * smooth[m]
             mine = mine + jnp.where(k == m, top, 0.0)
-        own = totals[k]
+        own = totals[g, k]
         for q in range(8):
             mine = mine + coarse_ref[0, :, pl.ds(q, 1)] * own[q : q + 1]
         return mine
 
-    def precondition(t):
-        local = apply(neumann, lambda f: share[f] * r[f])
-        coarse = coarse_value()
+    def precondition(t, g):
+        local = apply(neumann, g, lambda f: share[f] * r[g, f])
+        coarse = coarse_value(g)
         for f in (2, 3, 0, 1):
             value = local(f)
             for i in range(2):
                 q = 2 * f + i
                 value = value + mean[q] * coarse[q : q + 1]
             value = share[f] * value
-            hout[t, f] = value
-            send_face(halo, t, f)
-
-    for f in (0, 1, 2, 3):
-        wait_face(halo, 0, f)
-        r[f] = assembled(0, f)
-    sum_end(0)
-    for d in range(1, rows):
-        coef_arrival(d).wait_recv()
-    for m in range(rows):
-        totals[m] = row_totals(0, m)
-    precondition(1)
+            hout[GROUPS * t + g, f] = value
+            send_face(halo, GROUPS * t + g, f)
+
+    for g in range(GROUPS):
+        for f in (0, 1, 2, 3):
+            wait_face(halo, g, f)
+            r[g, f] = assembled(g, f)
+        sum_end(g)
+        if g == 0:
+            for d in range(1, rows):
+                coef_arrival(d).wait_recv()
+        for m in range(rows):
+            totals[g, m] = row_totals(g, m)
+        precondition(1, g)
 
     arrivals[3].wait()
     arrivals[4].wait()
@@ -385,77 +413,85 @@
         value = dot16(eh, ch, NT) + (dot16(eh, cl, NT) + dot16(el, ch, NT))
         store_pair(schur, f, slice(None), value)
 
-    def fold(value):
-        return jnp.sum(value, axis=0, keepdims=True)
-
-    rz = None
-    pap = None
+    rz = [None] * GROUPS
+    pap = [None] * GROUPS
     for step in range(ITERS):
-        t = 1 + 2 * step
         last = step + 1 == ITERS
-        for f in (0, 1, 2, 3):
-            wait_face(halo, t, f)
-        back = apply(schur, lambda f: assembled(t, f))
-        dots = [jnp.zeros((1, width), F32) for _ in range(2 if step == 0 else 3)]
-        for f in (2, 3, 0, 1):
-            z = assembled(t, f)
-            value = diag[f] * z - back(f)
-            hout[t + 1, f] = value
-            dots[0] = dots[0] + 0.5 * fold(r[f] * z)
-            dots[1] = dots[1] + fold(z * value)
+        for g in range(GROUPS):
+            t = GROUPS * (1 + 2 * step) + g
+            u = t + GROUPS
+            s = GROUPS * (step + 1) + g
+            for f in (0, 1, 2, 3):
+                wait_face(halo, t, f)
+            back = apply(schur, g, lambda f: assembled(t, f))
+            dots = [jnp.zeros((1, width), F32) for _ in range(2 if step == 0 else 3)]
+            for f in (2, 3, 0, 1):
+                z = assembled(t, f)
+                value = diag[f] * z - back(f)
+                hout[u, f] = value
+                dots[0] = dots[0] + fold(0.5 * (r[g, f] * z))
+                dots[1] = dots[1] + fold(z * value)
+                if step > 0:
+                    dots[2] = dots[2] + fold(0.5 * (z * image[g, f]) + p[g, f] * value)
+            if last:
+                sum_begin(s, packed_tile(None, [jnp.zeros((1, width), F32)] * 4 + dots))
+            else:
+                sum_begin(s, constraint_tile(lambda f: hout[u, f], dots))
+            for f in (2, 3, 0, 1):
+                send_face(halo, u, f)
+        for g in range(GROUPS):
+            sum_middle(GROUPS * (step + 1) + g)
+        for g in range(GROUPS):
+            t = GROUPS * (1 + 2 * step) + g
+            u = t + GROUPS
+            s = GROUPS * (step + 1) + g
+            for f in (0, 1, 2, 3):
+                wait_face(halo, u, f)
+            sum_end(s)
+            new = dot_total(s, 4)
+            new_pap = dot_total(s, 5)
             if step > 0:
-                dots[2] = dots[2] + fold(0.5 * (z * image[f]) + p[f] * value)
-        if last:
-            sum_begin(step + 1, dot_tile(dots, [jnp.zeros((1, width), F32)] * 4))
-        else:
-            sum_begin(step + 1, constraint_tiles(lambda f: hout[t + 1, f], dots))
-        for f in (2, 3, 0, 1):
-            send_face(halo, t + 1, f)
-        sum_middle(step + 1)
-        for f in (0, 1, 2, 3):
-            wait_face(halo, t + 1, f)
-        sum_end(step + 1)
-        new = dot_total(step + 1, 12)
-        new_pap = dot_total(step + 1, 13)
-        if step > 0:
-            beta = new / rz
-            new_pap = new_pap + beta * (dot_total(step + 1, 14) + beta * pap)
-        rz, pap = new, new_pap
-        alpha = rz / pap
-        for f in range(4):
-            z = assembled(t, f)
-            w = assembled(t + 1, f)
-            if step > 0:
-                z = z + beta * p[f]
-                w = w + beta * image[f]
-            p[f] = z
-            image[f] = w
-            x[f] = alpha * z if step == 0 else x[f] + alpha * z
-            r[f] = r[f] - alpha * w
-        if not last:
-            for m in range(rows):
-                value = row_totals(step + 1, m)
+                beta = new / rz[g]
+                new_pap = new_pap + beta * (dot_total(s, 6) + beta * pap[g])
+            rz[g], pap[g] = new, new_pap
+            alpha = new / new_pap
+            for f in range(4):
+                z = assembled(t, f)
+                w = assembled(u, f)
                 if step > 0:
-                    value = value + beta * moved[m]
-                moved[m] = value
-                totals[m] = totals[m] - alpha * value
-            precondition(t + 2)
+                    z = z + beta * p[g, f]
+                    w = w + beta * image[g, f]
+                p[g, f] = z
+                image[g, f] = w
+                x[g, f] = alpha * z if step == 0 else x[g, f] + alpha * z
+                r[g, f] = r[g, f] - alpha * w
+            if not last:
+                for m in range(rows):
+                    value = row_totals(s, m)
+                    if step > 0:
+                        value = value + beta * moved[g, m]
+                    moved[g, m] = value
+                    totals[g, m] = totals[g, m] - alpha * value
+                precondition(1 + 2 * (step + 1), g)
 
     for f in range(4):
         span = pl.ds(f * width, width)
         one = pick(f)
         for ref, field in ((x_out, x), (r_out, r)):
+            first, second = field[0, f], field[1, f]
+            top = jnp.where(low_lanes, first, roll(second))
+            bottom = jnp.where(low_lanes, roll(first), second)
             ref[0, 0, :, span] = jnp.dot(
-                field[f].T, one, precision=lax.Precision.HIGHEST, preferred_element_type=F32
+                jnp.concatenate([top, bottom], axis=0).T, one, precision=lax.Precision.HIGHEST, preferred_element_type=F32
             )
 
     for f in range(4):
         done_face(tiles, 0, f)
-        for t in range(HALOS):
+        for t in range(GROUPS * HALOS):
             done_face(halo, t, f)
     for d in range(1, rows):
         coef_copy(d).wait_send()
-    for t in range(SUMS):
+    for t in range(GROUPS * SUMS):
         for d in range(1, cols):
             circ_copy(t, d).wait_send()
         for d in range(1, rows):
@@ -467,41 +503,42 @@
     count, points = load.shape[2:]
     width = points // 4
     dma = pltpu.SemaphoreType.DMA
-    face = (4, width, width)
+    half = (4, width // GROUPS, width)
+    halos, sums = GROUPS * HALOS, GROUPS * SUMS
     scratch = [pltpu.VMEM(arg.shape, arg.dtype) for arg in args] + [
         dma((len(args),)),
-        pltpu.VMEM((HALOS,) + face, F32),
-        pltpu.VMEM((HALOS,) + face, F32),
+        pltpu.VMEM((halos,) + half, F32),
+        pltpu.VMEM((halos,) + half, F32),
         pltpu.VMEM((1, 4, 8, width), F32),
         pltpu.VMEM((1, 4, 8, width), F32),
-        pltpu.VMEM((SUMS, 16, width), F32),
-        pltpu.VMEM((SUMS, cols, 16, width), F32),
-        pltpu.VMEM((SUMS, rows, 16, width), F32),
+        pltpu.VMEM((sums, 8, width), F32),
+        pltpu.VMEM((sums, cols, 8, width), F32),
+        pltpu.VMEM((sums, rows, 8, width), F32),
         pltpu.VMEM((rows, 2, 8, width), F32),
-        pltpu.VMEM(face, BF16),
+        pltpu.VMEM((4, width, width), BF16),
         pltpu.VMEM((4, 2 * width, points), BF16),
         pltpu.VMEM((4, 2 * width, points), BF16),
         pltpu.VMEM((4, points, args[3].shape[-1]), BF16),
-        pltpu.VMEM((points, 2 * width), BF16),
-        pltpu.VMEM(face, F32),
-        pltpu.VMEM(face, F32),
-        pltpu.VMEM((8, width, width), F32),
-        pltpu.VMEM((8, width, width), F32),
-        pltpu.VMEM((8, width, width), F32),
-        pltpu.VMEM(face, F32),
-        pltpu.VMEM(face, F32),
-        pltpu.VMEM(face, F32),
-        pltpu.VMEM(face, F32),
-        pltpu.VMEM((rows, 8, width), F32),
-        pltpu.VMEM((rows, 8, width), F32),
-        dma((HALOS, 4)),
-        dma((HALOS, 4)),
+        pltpu.VMEM((GROUPS, points, width), BF16),
+        pltpu.VMEM(half, F32),
+        pltpu.VMEM(half, F32),
+        pltpu.VMEM((8,) + half[1:], F32),
+        pltpu.VMEM((8,) + half[1:], F32),
+        pltpu.VMEM((8,) + half[1:], F32),
+        pltpu.VMEM((GROUPS,) + half, F32),
+        pltpu.VMEM((GROUPS,) + half, F32),
+        pltpu.VMEM((GROUPS,) + half, F32),
+        pltpu.VMEM((GROUPS,) + half, F32),
+        pltpu.VMEM((GROUPS, rows, 8, width), F32),
+        pltpu.VMEM((GROUPS, rows, 8, width), F32),
+        dma((halos, 4)),
+        dma((halos, 4)),
         dma((1, 4)),
         dma((1, 4)),
-        dma((SUMS, cols)),
-        dma((SUMS, cols)),
-        dma((SUMS, rows)),
-        dma((SUMS, rows)),
+        dma((sums, cols)),
+        dma((sums, cols)),
+        dma((sums, rows)),
+        dma((sums, rows)),
         dma((rows,)),
         dma((rows,)),
     ]

time: 61.4 us -> 61.7 us (level)
  no operation moved by 1% of the time
where the time goes in v3:
time: 61.7 us; the launch traced here: 61.5 us
  Pallas kernels  58.5 us (95%)
  local copies, waits for them, and re-layouts  2.42 us (4%)
  between operations  0.65 us (1%)
    pallas_call x1, Pallas kernels, local(): pl.pallas_call(functools.partial(kernel, rows, cols), out_shape=(shape, s...  58.5 us
    unnamed x4, local copies, waits for them, and re-layouts  2.42 us

profile of v3, /device:TPU:0, one launch (start us, length us, event | category | flops | bytes accessed | tf_op | source)
XLA Modules:
  0.0 61.5 jit_solution(6826518466791871121)
XLA Ops:
  0.6 58.5 %shard_map.122 = (f32[1,1,128,512]{3,2,1,0:T(8,128)}, f32[1,1,128,512]{3,2,1,0:T(8,128)}) custom-call(f32[1,1,128,512]{3,2,1,0:T(8,128)} %refs_0_.1, f32[1,1,512]{2,1,0:T(1,128)} %refs_1_.1, f32[1,1,512]{2,1,0:T(1,128)} %refs_2_.1, f32[1,1,512,512]{3,2,1,0:T(8,128)} %refs_3_.1, f32[1,1,4,128,128]{4,3,2,1,0:T(8,128)} %refs_4_.1, f32[1,1,512,512]{3,2,1,0:T(8,128)} %refs_5_.1, ...), custom_call_target="tpu_custom_call" | custom-call | tf_op jit(solution)/shard_map/pallas_call | solution.py:546
  59.1 0.0 copy-start
  59.1 1.7 %copy.15 = f32[1,1,128,512]{3,2,1,0:T(8,128)} copy(f32[1,1,128,512]{3,2,1,0:T(8,128)} %get-tuple-element.4) | data formatting | bytes 524288
  60.8 0.0 copy-done
  60.8 0.7 %copy.16 = f32[1,1,128,512]{3,2,1,0:T(8,128)} copy(f32[1,1,128,512]{3,2,1,0:T(8,128)S(1)} %copy-done) | data formatting | bytes 524288
Async XLA Ops:
  59.1 1.7 %copy-start = (f32[1,1,128,512]{3,2,1,0:T(8,128)S(1)}, f32[1,1,128,512]{3,2,1,0:T(8,128)}, u32[]{:S(2)}) copy-start(f32[1,1,128,512]{3,2,1,0:T(8,128)} %get-tuple-element.5) | copy-start | bytes 786436

commit v4 on v2

--- a/solution.py
+++ b/solution.py
@@ -19,6 +19,13 @@
 def split(value):
     high = value.astype(BF16)
     return high, (value - high.astype(F32)).astype(BF16)
+
+
+def split3(value):
+    high = value.astype(BF16)
+    rest = value - high.astype(F32)
+    middle = rest.astype(BF16)
+    return high, middle, (rest - middle.astype(F32)).astype(BF16)
 
 
 def dot16(a, b, dims=(((1,), (0,)), ((), ()))):
@@ -38,7 +45,7 @@
         coarse_ref, lower_ref, upper_ref, order_ref, lists_ref,
     ) = held
     (
-        hout, hin, tile_out, tile_in, c_out, c_in, a_in, coef_in, perm, schur, neumann, half, vbuf,
+        hout, hin, tile_out, tile_in, c_out, c_in, a_in, coef_in, perm, schur, neumann, half, vbuf, wide, wide_t, inner, turned,
         share, diag, mean, own_w, near_w, x, r, p, image, totals, moved,
         hs, hr, ts, tr, cs, cr, as_, ar, fs, fr,
     ) = refs
@@ -119,16 +126,20 @@
     def spread(column):
         return jnp.broadcast_to(column, (width, width))
 
-    def pick(f):
-        return perm[f].astype(F32)
-
     for i in (9, 1, 2, 10, 0):
         arrivals[i].wait()
+
+    wide[...] = jnp.zeros_like(wide)
+    wide_t[...] = jnp.zeros_like(wide_t)
+    inner[...] = jnp.zeros_like(inner)
 
     for f in range(4):
         span = pl.ds(f * width, width)
         one = (order_ref[0, :, span] - f * width == sub).astype(F32)
         perm[f] = one.astype(BF16)
+        corner = pl.ds((f % 2) * width, width)
+        wide[f // 2, corner, corner] = one.astype(BF16)
+        wide_t[f // 2, corner, corner] = one.T.astype(BF16)
         rho = jnp.sum(one * rho_ref[0, :, span], axis=1, keepdims=True)
         dia = jnp.sum(one * diag_ref[0, :, span], axis=1, keepdims=True)
         diag[f] = spread(dia)
@@ -145,13 +156,9 @@
             lane == 0, rho, jnp.where(lane == 1, pair[:, 0:1], jnp.where(lane == 2, pair[:, 1:2], 0.0))
         )
         tile_out[0, f] = packed.T[0:8]
-        hout[0, f] = lax.dot_general(
-            one,
-            load_ref[0, 0, :, span],
-            NT,
-            precision=lax.Precision.HIGHEST,
-            preferred_element_type=F32,
-        )
+        full = dot16(perm[f], jnp.concatenate(split3(load_ref[0, 0, :, span].T), axis=1))
+        tail = full[:, width : 2 * width] + full[:, 2 * width :]
+        hout[0, f] = full[:, :width] + tail
 
     pl.semaphore_wait(barrier, rows + cols - 2)
     for f in (2, 3, 0, 1):
@@ -293,16 +300,20 @@
         table[f, pl.ds(0, width), cut] = high
         table[f, pl.ds(width, width), cut] = low
 
-    for f in range(4):
-        rows_f = pl.ds(f * width, width)
-        high, low = split(neumann_ref[0, 0, rows_f, :])
-        high = dot16(perm[f], high).astype(BF16)
-        low = dot16(perm[f], low).astype(BF16)
-        for g in range(4):
-            cut = slice(g * width, (g + 1) * width)
-            span = pl.ds(g * width, width)
-            neumann[f, pl.ds(0, width), span] = dot16(high[:, cut], perm[g], NT).astype(BF16)
-            neumann[f, pl.ds(width, width), span] = dot16(low[:, cut], perm[g], NT).astype(BF16)
+    points = 4 * width
+    pair = 2 * width
+    high, low = split(neumann_ref[0, 0])
+    for a in range(2):
+        cut = slice(a * pair, (a + 1) * pair)
+        for i, part in enumerate((high, low)):
+            turned[pl.ds(i * points, points), pl.ds(a * pair, pair)] = dot16(
+                part[:, cut], wide_t[a]
+            ).astype(BF16)
+    for a in range(2):
+        for i in range(2):
+            done = dot16(wide[a], turned[pl.ds(i * points + a * pair, pair), :]).astype(BF16)
+            for j in range(2):
+                neumann[2 * a + j, pl.ds(i * width, width), :] = done[j * width : (j + 1) * width]
 
     sum_middle(0)
 
@@ -366,24 +377,26 @@
     arrivals[3].wait()
     arrivals[4].wait()
 
-    for f in range(4):
-        span = pl.ds(f * width, width)
-        high, low = split(couple_ref[0, 0, span, :])
-        half[0, span, :] = dot16(perm[f], high).astype(BF16)
-        half[1, span, :] = dot16(perm[f], low).astype(BF16)
+    high, low = split(couple_ref[0, 0])
+    for a in range(2):
+        cut = slice(a * pair, (a + 1) * pair)
+        for i, part in enumerate((high, low)):
+            half[i, pl.ds(a * pair, pair), :] = dot16(wide[a], part[cut]).astype(BF16)
     for n in range(blocks_ref.shape[2]):
-        cut = pl.ds(n * block, block)
-        ih, il = split(blocks_ref[0, 0, n])
+        corner = pl.ds((n % 2) * block, block)
+        for i, part in enumerate(split(blocks_ref[0, 0, n])):
+            inner[i, n // 2, corner, corner] = part
+    for a in range(2):
+        cut = pl.ds(a * pair, pair)
         ch, cl = half[0, :, cut], half[1, :, cut]
+        ih, il = inner[0, a], inner[1, a]
         high, low = split(dot16(ch, ih) + (dot16(ch, il) + dot16(cl, ih)))
         half[2, :, cut] = high
         half[3, :, cut] = low
+    both = dot16(half[pl.ds(2, 2)].reshape(2 * points, points), half[0], NT)
+    value = both[:points] + (both[points:] + dot16(half[2], half[1], NT))
     for f in range(4):
-        span = pl.ds(f * width, width)
-        eh, el = half[2, span, :], half[3, span, :]
-        ch, cl = half[0], half[1]
-        value = dot16(eh, ch, NT) + (dot16(eh, cl, NT) + dot16(el, ch, NT))
-        store_pair(schur, f, slice(None), value)
+        store_pair(schur, f, slice(None), value[f * width : (f + 1) * width])
 
     def fold(value):
         return jnp.sum(value, axis=0, keepdims=True)
@@ -443,11 +456,11 @@
 
     for f in range(4):
         span = pl.ds(f * width, width)
-        one = pick(f)
-        for ref, field in ((x_out, x), (r_out, r)):
-            ref[0, 0, :, span] = jnp.dot(
-                field[f].T, one, precision=lax.Precision.HIGHEST, preferred_element_type=F32
-            )
+        parts = split3(x[f].T) + split3(r[f].T)
+        full = dot16(jnp.concatenate(parts, axis=0), perm[f])
+        full = [full[i * width : (i + 1) * width] for i in range(6)]
+        x_out[0, 0, :, span] = full[0] + (full[1] + full[2])
+        r_out[0, 0, :, span] = full[3] + (full[4] + full[5])
 
     for f in range(4):
         done_face(tiles, 0, f)
@@ -483,6 +496,10 @@
         pltpu.VMEM((4, 2 * width, points), BF16),
         pltpu.VMEM((4, points, args[3].shape[-1]), BF16),
         pltpu.VMEM((points, 2 * width), BF16),
+        pltpu.VMEM((2, 2 * width, 2 * width), BF16),
+        pltpu.VMEM((2, 2 * width, 2 * width), BF16),
+        pltpu.VMEM((2, 2, 2 * width, 2 * width), BF16),
+        pltpu.VMEM((2 * points, points), BF16),
         pltpu.VMEM(face, F32),
         pltpu.VMEM(face, F32),
         pltpu.VMEM((8, width, width), F32),

time: 61.4 us -> 61.2 us (level)
  no operation moved by 1% of the time
where the time goes in v4:
time: 61.2 us; the launch traced here: 61 us
  Pallas kernels  57.9 us (95%)
  local copies, waits for them, and re-layouts  2.42 us (4%)
  between operations  0.65 us (1%)
    pallas_call x1, Pallas kernels, local(): pl.pallas_call(functools.partial(kernel, rows, cols), out_shape=(shape, s...  57.9 us
    unnamed x4, local copies, waits for them, and re-layouts  2.42 us

profile of v4, /device:TPU:0, one launch (start us, length us, event | category | flops | bytes accessed | tf_op | source)
XLA Modules:
  0.0 61.0 jit_solution(12844849133580387459)
XLA Ops:
  0.6 57.9 %shard_map.122 = (f32[1,1,128,512]{3,2,1,0:T(8,128)}, f32[1,1,128,512]{3,2,1,0:T(8,128)}) custom-call(f32[1,1,128,512]{3,2,1,0:T(8,128)} %refs_0_.1, f32[1,1,512]{2,1,0:T(1,128)} %refs_1_.1, f32[1,1,512]{2,1,0:T(1,128)} %refs_2_.1, f32[1,1,512,512]{3,2,1,0:T(8,128)} %refs_3_.1, f32[1,1,4,128,128]{4,3,2,1,0:T(8,128)} %refs_4_.1, f32[1,1,512,512]{3,2,1,0:T(8,128)} %refs_5_.1, ...), custom_call_target="tpu_custom_call" | custom-call | tf_op jit(solution)/shard_map/pallas_call | solution.py:526
  58.6 0.0 copy-start
  58.6 1.7 %copy.15 = f32[1,1,128,512]{3,2,1,0:T(8,128)} copy(f32[1,1,128,512]{3,2,1,0:T(8,128)} %get-tuple-element.4) | data formatting | bytes 524288
  60.3 0.0 copy-done
  60.3 0.7 %copy.16 = f32[1,1,128,512]{3,2,1,0:T(8,128)} copy(f32[1,1,128,512]{3,2,1,0:T(8,128)S(1)} %copy-done) | data formatting | bytes 524288
Async XLA Ops:
  58.6 1.7 %copy-start = (f32[1,1,128,512]{3,2,1,0:T(8,128)S(1)}, f32[1,1,128,512]{3,2,1,0:T(8,128)}, u32[]{:S(2)}) copy-start(f32[1,1,128,512]{3,2,1,0:T(8,128)} %get-tuple-element.5) | copy-start | bytes 786436

commit v5 on v4

--- a/solution.py
+++ b/solution.py
@@ -422,9 +422,11 @@
             sum_begin(step + 1, dot_tile(dots, [jnp.zeros((1, width), F32)] * 4))
         else:
             sum_begin(step + 1, constraint_tiles(lambda f: hout[t + 1, f], dots))
-        for f in (2, 3, 0, 1):
+        for f in (2, 3):
             send_face(halo, t + 1, f)
         sum_middle(step + 1)
+        for f in (0, 1):
+            send_face(halo, t + 1, f)
         for f in (0, 1, 2, 3):
             wait_face(halo, t + 1, f)
         sum_end(step + 1)

time: 61.2 us -> 61.3 us (level)
  no operation moved by 1% of the time
where the time goes in v5:
time: 61.3 us; the launch traced here: 61.1 us
  Pallas kernels  58.1 us (95%)
  local copies, waits for them, and re-layouts  2.42 us (4%)
  between operations  0.65 us (1%)
    pallas_call x1, Pallas kernels, local(): pl.pallas_call(functools.partial(kernel, rows, cols), out_shape=(shape, s...  58.1 us
    unnamed x4, local copies, waits for them, and re-layouts  2.42 us

profile of v5, /device:TPU:0, one launch (start us, length us, event | category | flops | bytes accessed | tf_op | source)
XLA Modules:
  0.0 61.1 jit_solution(16290881792177675149)
XLA Ops:
  0.6 58.1 %shard_map.122 = (f32[1,1,128,512]{3,2,1,0:T(8,128)}, f32[1,1,128,512]{3,2,1,0:T(8,128)}) custom-call(f32[1,1,128,512]{3,2,1,0:T(8,128)} %refs_0_.1, f32[1,1,512]{2,1,0:T(1,128)} %refs_1_.1, f32[1,1,512]{2,1,0:T(1,128)} %refs_2_.1, f32[1,1,512,512]{3,2,1,0:T(8,128)} %refs_3_.1, f32[1,1,4,128,128]{4,3,2,1,0:T(8,128)} %refs_4_.1, f32[1,1,512,512]{3,2,1,0:T(8,128)} %refs_5_.1, ...), custom_call_target="tpu_custom_call" | custom-call | tf_op jit(solution)/shard_map/pallas_call | solution.py:528
  58.7 0.0 copy-start
  58.7 1.7 %copy.15 = f32[1,1,128,512]{3,2,1,0:T(8,128)} copy(f32[1,1,128,512]{3,2,1,0:T(8,128)} %get-tuple-element.4) | data formatting | bytes 524288
  60.4 0.0 copy-done
  60.4 0.7 %copy.16 = f32[1,1,128,512]{3,2,1,0:T(8,128)} copy(f32[1,1,128,512]{3,2,1,0:T(8,128)S(1)} %copy-done) | data formatting | bytes 524288
Async XLA Ops:
  58.7 1.7 %copy-start = (f32[1,1,128,512]{3,2,1,0:T(8,128)S(1)}, f32[1,1,128,512]{3,2,1,0:T(8,128)}, u32[]{:S(2)}) copy-start(f32[1,1,128,512]{3,2,1,0:T(8,128)} %get-tuple-element.5) | copy-start | bytes 786436
